TPU v7x, 32 devices: a whole 2x2x4 slice. The times are simulated.
32 devices in a mesh: seq: 8 (over y, x, core), chan: 4 (over z).
Axes of the slice: x: 2, y: 2, z: 4, core: 2. Of those that a mesh axis runs over, the one named last changes fastest.
Arguments:
- tokens: float32 [6, 4096, 1024], P(None, 'seq'), may hold values from -6 to 6
- segment_ids: int32 [6, 4096], P(None, 'seq'), may hold values from 0 to 4095, as said below
- cotangent: float32 [6, 4096, 1024], P(None, 'seq'), may hold values from -6 to 6
- norm_gains: float32 [2, 1024], replicated, may hold values from 0.5 to 1.5
- filter_weight: float32 [3, 1024], P(None, 'chan'), may hold values from -0.6 to 0.6
- in_weight: float32 [1024, 3, 1024], P('seq', None, 'chan'), may hold values from -0.1875 to 0.1875
- out_weight: float32 [1024, 1024], P('seq', 'chan'), may hold values from -0.1875 to 0.1875
- gate_weight: float32 [1024, 4608], P('seq', 'chan'), may hold values from -0.1875 to 0.1875
- up_weight: float32 [1024, 4608], P('seq', 'chan'), may hold values from -0.1875 to 0.1875
- down_weight: float32 [1024, 4608], P('seq', 'chan'), may hold values from -0.09375 to 0.09375
- norm_gains_mean: float32 [2, 1024], replicated
- norm_gains_square: float32 [2, 1024], replicated
- filter_mean: float32 [3, 1024], P(None, 'chan')
- filter_square: float32 [3, 1024], P(None, 'chan')
- in_momentum: float32 [1024, 3, 1024], P('seq', None, 'chan')
- out_momentum: float32 [1024, 1024], P('seq', 'chan')
- gate_momentum: float32 [1024, 4608], P('seq', 'chan')
- up_momentum: float32 [1024, 4608], P('seq', 'chan')
- down_momentum: float32 [1024, 4608], P('seq', 'chan')
Outputs:
- block_out: float32 [6, 4096, 1024], P(None, 'seq')
- input_grad: float32 [6, 4096, 1024], P(None, 'seq')
- norm_gains_new: float32 [2, 1024], replicated
- norm_gains_mean_new: float32 [2, 1024], replicated
- norm_gains_square_new: float32 [2, 1024], replicated
- filter_new: float32 [3, 1024], P(None, 'chan')
- filter_mean_new: float32 [3, 1024], P(None, 'chan')
- filter_square_new: float32 [3, 1024], P(None, 'chan')
- in_momentum_new: float32 [1024, 3, 1024], P('seq', None, 'chan')
- in_weight_new: float32 [1024, 3, 1024], P('seq', None, 'chan')
- out_momentum_new: float32 [1024, 1024], P('seq', 'chan')
- out_weight_new: float32 [1024, 1024], P('seq', 'chan')
- gate_momentum_new: float32 [1024, 4608], P('seq', 'chan')
- gate_weight_new: float32 [1024, 4608], P('seq', 'chan')
- up_momentum_new: float32 [1024, 4608], P('seq', 'chan')
- up_weight_new: float32 [1024, 4608], P('seq', 'chan')
- down_momentum_new: float32 [1024, 4608], P('seq', 'chan')
- down_weight_new: float32 [1024, 4608], P('seq', 'chan')
Inputs may be any that keep to these rules, and one draw needn't show every extreme that they name: `segment_ids`: in each sequence, a token's id is the position (from 0) at which its document begins: ids never fall, each id is at most its position, and a token whose id equals its position begins a document. One sequence, drawn afresh, is a single document.
All inputs are finite; a program needn't handle non-finite values.
Results may differ from a plain program's by a relative error of at most 0.018.
Values may be sent and summed in bfloat16 or wider, within the bound.
A program may use at most 256 MiB of HBM per device.

v0:
```python
import math

import jax
import jax.numpy as jnp
from jax import lax
from jax.sharding import PartitionSpec as P

D = 1024
FF = 4608
NS_ITERS = 4
STEP = 10


NORM_EPS = 1e-05
QUINTIC_FIRST = 3.4445
QUINTIC_SECOND = -4.775
QUINTIC_THIRD = 2.0315
MOMENTUM_DECAY = 0.95
FIRST_DECAY = 0.9
SECOND_DECAY = 0.999
ADAM_EPS = 1e-08
ADAM_RATE = 0.4
WEIGHT_DECAY = 0.01
ORTHO_EPS = 1e-07


def shifted(value, axis, by):
    length = lax.axis_size(axis)
    pairs = [(i, i + by) for i in range(length) if 0 <= i + by < length]
    return lax.ppermute(value, axis, pairs)


def contract_rows(left, right):
    return lax.dot_general(
        left, right, (((0,), (0,)), ((), ())), preferred_element_type=jnp.float32
    )


def contract_last(left, right):
    return lax.dot_general(
        left, right, (((1,), (1,)), ((), ())), preferred_element_type=jnp.float32
    )


def adam_update(param, gradient, first, second):
    first_new = FIRST_DECAY * first + (1.0 - FIRST_DECAY) * gradient
    second_new = SECOND_DECAY * second + (1.0 - SECOND_DECAY) * gradient * gradient
    first_fix = 1.0 - FIRST_DECAY**STEP
    second_fix = 1.0 - SECOND_DECAY**STEP
    param_new = param - ADAM_RATE * (first_new / first_fix) / (
        jnp.sqrt(second_new / second_fix) + ADAM_EPS
    )
    return (param_new, first_new, second_new)


def on_device(
    tokens,
    segment_ids,
    cotangent,
    norm_gains,
    filter_weight,
    in_weight,
    out_weight,
    gate_weight,
    up_weight,
    down_weight,
    norm_gains_mean,
    norm_gains_square,
    filter_mean,
    filter_square,
    in_momentum,
    out_momentum,
    gate_momentum,
    up_momentum,
    down_momentum,
):
    seq_place = lax.axis_index("seq")
    seq_total, local_rows, model_width = tokens.shape
    token_count = seq_total * local_rows
    chan_width = filter_weight.shape[1]
    in_full, out_full, gate_full, up_full, down_full = (
        lax.all_gather(in_weight.astype(jnp.bfloat16), "seq", axis=0, tiled=True),
        lax.all_gather(out_weight.astype(jnp.bfloat16), "seq", axis=0, tiled=True),
        lax.all_gather(gate_weight.astype(jnp.bfloat16), "seq", axis=0, tiled=True),
        lax.all_gather(up_weight.astype(jnp.bfloat16), "seq", axis=0, tiled=True),
        lax.all_gather(down_weight.astype(jnp.bfloat16), "seq", axis=0, tiled=True),
    )
    in_flat = in_full.reshape(model_width, 3 * chan_width)
    flat_tokens = tokens.reshape(token_count, model_width)
    first_scale = lax.rsqrt(jnp.mean(flat_tokens * flat_tokens, axis=1, keepdims=True) + NORM_EPS)
    first_unit = flat_tokens * first_scale
    first_normed = (first_unit * norm_gains[0]).astype(jnp.bfloat16)
    streams = jnp.dot(first_normed, in_flat, preferred_element_type=jnp.float32)
    streams = streams.reshape(seq_total, local_rows, 3, chan_width)
    input_gate = streams[:, :, 0]
    output_gate = streams[:, :, 1]
    value_stream = streams[:, :, 2]
    gated_input = input_gate * value_stream
    halo_rows = shifted(gated_input[:, local_rows - 2 :], "seq", 1)
    extended = jnp.concatenate([halo_rows, gated_input], axis=1)
    positions = seq_place * local_rows + jnp.arange(local_rows, dtype=jnp.int32)
    keep_masks = [None]
    for offset in (1, 2):
        keep_masks.append(
            (segment_ids <= positions[None, :] - offset).astype(jnp.float32)[:, :, None]
        )
    filtered = filter_weight[2] * gated_input
    for offset in (1, 2):
        filtered = (
            filtered
            + filter_weight[2 - offset]
            * keep_masks[offset]
            * extended[:, 2 - offset : 2 - offset + local_rows]
        )
    mixer_input = (output_gate * filtered).reshape(token_count, chan_width).astype(jnp.bfloat16)
    mixer_out = lax.psum(contract_last(mixer_input, out_full).astype(jnp.bfloat16), "chan").astype(
        jnp.float32
    )
    residual = flat_tokens + mixer_out
    second_scale = lax.rsqrt(jnp.mean(residual * residual, axis=1, keepdims=True) + NORM_EPS)
    second_unit = residual * second_scale
    second_normed = (second_unit * norm_gains[1]).astype(jnp.bfloat16)
    gate_value = jnp.dot(second_normed, gate_full, preferred_element_type=jnp.float32)
    up_value = jnp.dot(second_normed, up_full, preferred_element_type=jnp.float32)
    sigmoid_value = jax.nn.sigmoid(gate_value)
    silu_value = gate_value * sigmoid_value
    activated = (silu_value * up_value).astype(jnp.bfloat16)
    ffn_out = lax.psum(contract_last(activated, down_full).astype(jnp.bfloat16), "chan").astype(
        jnp.float32
    )
    block_out = (residual + ffn_out).reshape(tokens.shape)
    upstream = cotangent.reshape(token_count, model_width)
    upstream_low = upstream.astype(jnp.bfloat16)
    down_weight_grad = contract_rows(upstream_low, activated)
    act_grad = jnp.dot(upstream_low, down_full, preferred_element_type=jnp.float32)
    gate_low = (
        act_grad * up_value * sigmoid_value * (1.0 + gate_value * (1.0 - sigmoid_value))
    ).astype(jnp.bfloat16)
    up_low = (act_grad * silu_value).astype(jnp.bfloat16)
    gate_weight_grad = contract_rows(second_normed, gate_low)
    up_weight_grad = contract_rows(second_normed, up_low)
    second_part = contract_last(gate_low, gate_full) + contract_last(up_low, up_full)
    second_grad = lax.psum(second_part.astype(jnp.bfloat16), "chan").astype(jnp.float32)
    second_gain_grad = jnp.sum(second_grad * second_unit, axis=0)
    second_scaled = second_grad * norm_gains[1]
    residual_grad = upstream + second_scale * (
        second_scaled - second_unit * jnp.mean(second_scaled * second_unit, axis=1, keepdims=True)
    )
    residual_low = residual_grad.astype(jnp.bfloat16)
    out_weight_grad = contract_rows(residual_low, mixer_input)
    mixer_grad = jnp.dot(residual_low, out_full, preferred_element_type=jnp.float32).reshape(
        seq_total, local_rows, chan_width
    )
    output_gate_grad = mixer_grad * filtered
    filter_grad_in = mixer_grad * output_gate
    extended_grad = jnp.pad(filter_weight[2] * filter_grad_in, ((0, 0), (2, 0), (0, 0)))
    tap_grads = [jnp.sum(filter_grad_in * gated_input, axis=(0, 1))]
    for offset in (1, 2):
        masked_grad = keep_masks[offset] * filter_grad_in
        extended_grad = extended_grad + jnp.pad(
            filter_weight[2 - offset] * masked_grad, ((0, 0), (2 - offset, offset), (0, 0))
        )
        tap_grads.append(
            jnp.sum(masked_grad * extended[:, 2 - offset : 2 - offset + local_rows], axis=(0, 1))
        )
    filter_grad = jnp.stack([tap_grads[2], tap_grads[1], tap_grads[0]])
    returned = shifted(extended_grad[:, :2], "seq", -1)
    gated_grad = extended_grad[:, 2:] + jnp.pad(returned, ((0, 0), (local_rows - 2, 0), (0, 0)))
    stream_grad = jnp.stack(
        [gated_grad * value_stream, output_gate_grad, gated_grad * input_gate], axis=2
    )
    stream_grad = stream_grad.reshape(token_count, 3 * chan_width).astype(jnp.bfloat16)
    in_weight_grad = contract_rows(first_normed, stream_grad).reshape(model_width, 3, chan_width)
    first_grad = lax.psum(contract_last(stream_grad, in_flat).astype(jnp.bfloat16), "chan").astype(
        jnp.float32
    )
    first_gain_grad = jnp.sum(first_grad * first_unit, axis=0)
    first_scaled = first_grad * norm_gains[0]
    input_grad = residual_grad + first_scale * (
        first_scaled - first_unit * jnp.mean(first_scaled * first_unit, axis=1, keepdims=True)
    )
    input_grad = input_grad.reshape(tokens.shape)
    in_grad, out_grad, gate_grad, up_grad, down_grad = (
        lax.psum_scatter(
            in_weight_grad.astype(jnp.bfloat16), "seq", scatter_dimension=0, tiled=True
        ).astype(jnp.float32),
        lax.psum_scatter(
            out_weight_grad.astype(jnp.bfloat16), "seq", scatter_dimension=0, tiled=True
        ).astype(jnp.float32),
        lax.psum_scatter(
            gate_weight_grad.astype(jnp.bfloat16), "seq", scatter_dimension=0, tiled=True
        ).astype(jnp.float32),
        lax.psum_scatter(
            up_weight_grad.astype(jnp.bfloat16), "seq", scatter_dimension=0, tiled=True
        ).astype(jnp.float32),
        lax.psum_scatter(
            down_weight_grad.astype(jnp.bfloat16), "seq", scatter_dimension=0, tiled=True
        ).astype(jnp.float32),
    )
    gains_grad, filter_total = lax.psum(
        (jnp.stack([first_gain_grad, second_gain_grad]), filter_grad), "seq"
    )
    gains_new, gains_mean_new, gains_square_new = adam_update(
        norm_gains, gains_grad, norm_gains_mean, norm_gains_square
    )
    filter_new, filter_mean_new, filter_square_new = adam_update(
        filter_weight, filter_total, filter_mean, filter_square
    )
    weights = [in_weight, out_weight, gate_weight, up_weight, down_weight]
    gradients = [in_grad, out_grad, gate_grad, up_grad, down_grad]
    old_momenta = [in_momentum, out_momentum, gate_momentum, up_momentum, down_momentum]
    momenta = [MOMENTUM_DECAY * old_momenta[index] + gradients[index] for index in range(5)]
    flat_momenta = [moment.reshape(moment.shape[0], -1) for moment in momenta]
    rates = [1.0, 1.0, 1.0, 1.0, 0.5]
    column_totals = [3 * D, D, FF, FF, FF]
    squares = jnp.stack([jnp.sum(moment * moment) for moment in flat_momenta])
    totals = lax.psum(squares, ("seq", "chan"))
    states = [
        (flat_momenta[index] / (jnp.sqrt(totals[index]) + ORTHO_EPS)).astype(jnp.bfloat16)
        for index in range(5)
    ]
    for iteration in range(NS_ITERS):
        columns_all = (
            lax.all_gather(states[0], "seq", axis=0, tiled=True),
            lax.all_gather(states[1], "seq", axis=0, tiled=True),
            lax.all_gather(states[2], "seq", axis=0, tiled=True),
            lax.all_gather(states[3], "seq", axis=0, tiled=True),
            lax.all_gather(states[4], "seq", axis=0, tiled=True),
        )
        partial_value = [contract_last(states[index], columns_all[index]) for index in range(5)]
        grams = (
            lax.psum(partial_value[0].astype(jnp.bfloat16), "chan").astype(jnp.float32),
            lax.psum(partial_value[1].astype(jnp.bfloat16), "chan").astype(jnp.float32),
            lax.psum(partial_value[2].astype(jnp.bfloat16), "chan").astype(jnp.float32),
            lax.psum(partial_value[3].astype(jnp.bfloat16), "chan").astype(jnp.float32),
            lax.psum(partial_value[4].astype(jnp.bfloat16), "chan").astype(jnp.float32),
        )
        grams_low = [gram.astype(jnp.bfloat16) for gram in grams]
        grams_whole = (
            lax.all_gather(grams_low[0], "seq", axis=0, tiled=True),
            lax.all_gather(grams_low[1], "seq", axis=0, tiled=True),
            lax.all_gather(grams_low[2], "seq", axis=0, tiled=True),
            lax.all_gather(grams_low[3], "seq", axis=0, tiled=True),
            lax.all_gather(grams_low[4], "seq", axis=0, tiled=True),
        )
        next_states = []
        for index in range(5):
            square = jnp.dot(
                grams_low[index], grams_whole[index], preferred_element_type=jnp.float32
            )
            poly = (
                QUINTIC_SECOND * grams_low[index].astype(jnp.float32) + QUINTIC_THIRD * square
            ).astype(jnp.bfloat16)
            update = jnp.dot(poly, columns_all[index], preferred_element_type=jnp.float32)
            next_states.append(
                (QUINTIC_FIRST * states[index].astype(jnp.float32) + update).astype(jnp.bfloat16)
            )
        states = next_states
    own_pieces = [
        states[index].astype(jnp.float32).reshape(weights[index].shape) for index in range(5)
    ]
    new_weights = []
    for index in range(5):
        rate = rates[index]
        new_weights.append(
            weights[index] * (1.0 - WEIGHT_DECAY * rate)
            - rate * math.sqrt(column_totals[index] / D) * own_pieces[index]
        )
    return (
        block_out,
        input_grad,
        gains_new,
        gains_mean_new,
        gains_square_new,
        filter_new,
        filter_mean_new,
        filter_square_new,
        momenta[0],
        new_weights[0],
        momenta[1],
        new_weights[1],
        momenta[2],
        new_weights[2],
        momenta[3],
        new_weights[3],
        momenta[4],
        new_weights[4],
    )


def solution(mesh):
    return jax.shard_map(
        on_device,
        mesh=mesh,
        in_specs=(
            P(None, "seq", None),
            P(None, "seq"),
            P(None, "seq", None),
            P(),
            P(None, "chan"),
            P("seq", None, "chan"),
            P("seq", "chan"),
            P("seq", "chan"),
            P("seq", "chan"),
            P("seq", "chan"),
            P(),
            P(),
            P(None, "chan"),
            P(None, "chan"),
            P("seq", None, "chan"),
            P("seq", "chan"),
            P("seq", "chan"),
            P("seq", "chan"),
            P("seq", "chan"),
        ),
        out_specs=(
            P(None, "seq", None),
            P(None, "seq", None),
            P(),
            P(),
            P(),
            P(None, "chan"),
            P(None, "chan"),
            P(None, "chan"),
            P("seq", None, "chan"),
            P("seq", None, "chan"),
            P("seq", "chan"),
            P("seq", "chan"),
            P("seq", "chan"),
            P("seq", "chan"),
            P("seq", "chan"),
            P("seq", "chan"),
            P("seq", "chan"),
            P("seq", "chan"),
        ),
        check_vma=False,
    )
```

profile of v0, /device:TPU:0, one launch (start us, length us, event | category | flops | bytes accessed | tf_op | source)
XLA Modules:
  0.0 2688.9 jit_solution(6573960444140655715)
XLA Ops:
  23.5 15.6 all-gather.41.cloned.1.call-done
  81.7 210.0 %all-reduce.16.cloned.1.call-done = bf16[3072,1024]{1,0:T(8,128)(2,1)} async-done(((bf16[3072,1024]{1,0:T(8,128)(2,1)}), bf16[3072,1024]{1,0:T(8,128)(2,1)}) %all-reduce.16.cloned.1.call-update) | async-done | bytes 6291472 | tf_op jit(solution)/shard_map/psum | solution.py:116
  307.3 14.9 all-gather.43.cloned.1.call-done
  336.2 17.4 all-gather.45.cloned.1.call-done
  367.6 17.3 all-gather.47.cloned.1.call-done
  384.9 25.2 multiply_convert_fusion
  410.1 15.9 fusion.242
  486.5 174.8 %all-reduce.18.cloned.1.call-done = bf16[3072,1024]{1,0:T(8,128)(2,1)} async-done(((bf16[3072,1024]{1,0:T(8,128)(2,1)}), bf16[3072,1024]{1,0:T(8,128)(2,1)}) %all-reduce.18.cloned.1.call-update) | async-done | bytes 6291472 | tf_op jit(solution)/shard_map/psum | solution.py:143
  737.6 14.8 reduce-scatter.12.cloned.1.call-done
  754.1 44.2 %reduce-scatter.14.cloned.1.call-done = bf16[128,1152]{1,0:T(8,128)(2,1)} async-done(((bf16[1024,1152]{1,0:T(8,128)(2,1)}), bf16[128,1152]{1,0:T(8,128)(2,1)}) %reduce-scatter.14.cloned.1.call-update) | async-done | bytes 294928 | tf_op jit(solution)/shard_map/reduce_scatter | solution.py:196
  800.0 36.2 %reduce-scatter.8.cloned.1.call-done = bf16[128,256]{1,0:T(8,128)(2,1)} async-done(((bf16[1024,256]{1,0:T(8,128)(2,1)}), bf16[128,256]{1,0:T(8,128)(2,1)}) %reduce-scatter.8.cloned.1.call-update) | async-done | bytes 65552 | tf_op jit(solution)/shard_map/reduce_scatter | solution.py:187
  837.7 40.9 %reduce-scatter.6.cloned.1.call-done = bf16[128,3,256]{2,0,1:T(8,128)(2,1)} async-done(((bf16[1024,3,256]{2,0,1:T(8,128)(2,1)}), bf16[128,3,256]{2,0,1:T(8,128)(2,1)}) %reduce-scatter.6.cloned.1.call-update) | async-done | bytes 196624 | tf_op jit(solution)/shard_map/reduce_scatter | solution.py:184
  883.7 39.7 %psum.195 = f32[5]{0:T(128)S(1)} all-reduce(f32[5]{0:T(128)S(1)} %stack.67), channel_id=1, replica_groups=mesh['seq'=8,'chan'=4] {'seq','chan'}, use_global_device_ids=true, to_apply=%region_25.26 | all-reduce | flops 5 | bytes 40 | tf_op jit(solution)/shard_map/psum | solution.py:217
  955.9 29.0 %all-gather.105.cloned.1.call-done = bf16[1024,1152]{1,0:T(8,128)(2,1)} async-done(((bf16[128,1152]{1,0:T(8,128)(2,1)}), bf16[1024,1152]{1,0:T(8,128)(2,1)}) %all-gather.105.cloned.1.call-update) | async-done | bytes 2359312 | tf_op jit(solution)/shard_map/all_gather | solution.py:228
  988.2 28.1 %all-gather.89.cloned.1.call-done = bf16[1024,1152]{1,0:T(8,128)(2,1)} async-done(((bf16[128,1152]{1,0:T(8,128)(2,1)}), bf16[1024,1152]{1,0:T(8,128)(2,1)}) %all-gather.89.cloned.1.call-update) | async-done | bytes 2359312 | tf_op jit(solution)/shard_map/all_gather | solution.py:227
  1019.5 28.1 %all-gather.73.cloned.1.call-done = bf16[1024,1152]{1,0:T(8,128)(2,1)} async-done(((bf16[128,1152]{1,0:T(8,128)(2,1)}), bf16[1024,1152]{1,0:T(8,128)(2,1)}) %all-gather.73.cloned.1.call-update) | async-done | bytes 2359312 | tf_op jit(solution)/shard_map/all_gather | solution.py:226
  1051.0 62.6 %all-reduce.26.cloned.1.call-done = (bf16[128,1024]{1,0:T(8,128)(2,1)}, bf16[128,1024]{1,0:T(8,128)(2,1)}, bf16[128,1024]{1,0:T(8,128)(2,1)}, bf16[128,1024]{1,0:T(8,128)(2,1)}, bf16[128,1024]{1,0:T(8,128)(2,1)}) async-done(((bf16[128,1024]{1,0:T(8,128)(2,1)}, bf16[128,1024]{1,0:T(8,128)(2,1)}, bf16[128,1024]{1,0:T(8,128)(2,1)}, bf16[128,1024]{1,0:T(8,128)(2,1)}, bf16[128,1024]{1,0:T(8,128)(2,1)}), ...) | async-done | bytes 1310736 | tf_op jit(solution)/shard_map/psum | solution.py:232
  1117.1 25.1 all-gather.51.cloned.1.call-done
  1146.0 25.8 all-gather.107.cloned.1.call-done
  1175.1 26.6 all-gather.91.cloned.1.call-done
  1205.7 25.6 all-gather.75.cloned.1.call-done
  1234.6 26.6 all-gather.65.cloned.1.call-done
  1291.5 28.7 %all-gather.109.cloned.1.call-done = bf16[1024,1152]{1,0:T(8,128)(2,1)} async-done(((bf16[128,1152]{1,0:T(8,128)(2,1)}), bf16[1024,1152]{1,0:T(8,128)(2,1)}) %all-gather.109.cloned.1.call-update) | async-done | bytes 2359312 | tf_op jit(solution)/shard_map/all_gather | solution.py:228
  1323.5 28.1 %all-gather.93.cloned.1.call-done = bf16[1024,1152]{1,0:T(8,128)(2,1)} async-done(((bf16[128,1152]{1,0:T(8,128)(2,1)}), bf16[1024,1152]{1,0:T(8,128)(2,1)}) %all-gather.93.cloned.1.call-update) | async-done | bytes 2359312 | tf_op jit(solution)/shard_map/all_gather | solution.py:227
  1354.9 28.2 %all-gather.77.cloned.1.call-done = bf16[1024,1152]{1,0:T(8,128)(2,1)} async-done(((bf16[128,1152]{1,0:T(8,128)(2,1)}), bf16[1024,1152]{1,0:T(8,128)(2,1)}) %all-gather.77.cloned.1.call-update) | async-done | bytes 2359312 | tf_op jit(solution)/shard_map/all_gather | solution.py:226
  1386.5 62.6 %all-reduce.24.cloned.1.call-done = (bf16[128,1024]{1,0:T(8,128)(2,1)}, bf16[128,1024]{1,0:T(8,128)(2,1)}, bf16[128,1024]{1,0:T(8,128)(2,1)}, bf16[128,1024]{1,0:T(8,128)(2,1)}, bf16[128,1024]{1,0:T(8,128)(2,1)}) async-done(((bf16[128,1024]{1,0:T(8,128)(2,1)}, bf16[128,1024]{1,0:T(8,128)(2,1)}, bf16[128,1024]{1,0:T(8,128)(2,1)}, bf16[128,1024]{1,0:T(8,128)(2,1)}, bf16[128,1024]{1,0:T(8,128)(2,1)}), ...) | async-done | bytes 1310736 | tf_op jit(solution)/shard_map/psum | solution.py:232
  1451.9 25.7 all-gather.55.cloned.1.call-done
  1481.6 25.9 all-gather.111.cloned.1.call-done
  1510.8 26.5 all-gather.95.cloned.1.call-done
  1541.2 25.7 all-gather.79.cloned.1.call-done
  1570.2 26.6 all-gather.67.cloned.1.call-done
  1627.2 28.6 %all-gather.113.cloned.1.call-done = bf16[1024,1152]{1,0:T(8,128)(2,1)} async-done(((bf16[128,1152]{1,0:T(8,128)(2,1)}), bf16[1024,1152]{1,0:T(8,128)(2,1)}) %all-gather.113.cloned.1.call-update) | async-done | bytes 2359312 | tf_op jit(solution)/shard_map/all_gather | solution.py:228
  1659.0 28.3 %all-gather.97.cloned.1.call-done = bf16[1024,1152]{1,0:T(8,128)(2,1)} async-done(((bf16[128,1152]{1,0:T(8,128)(2,1)}), bf16[1024,1152]{1,0:T(8,128)(2,1)}) %all-gather.97.cloned.1.call-update) | async-done | bytes 2359312 | tf_op jit(solution)/shard_map/all_gather | solution.py:227
  1690.5 28.2 %all-gather.81.cloned.1.call-done = bf16[1024,1152]{1,0:T(8,128)(2,1)} async-done(((bf16[128,1152]{1,0:T(8,128)(2,1)}), bf16[1024,1152]{1,0:T(8,128)(2,1)}) %all-gather.81.cloned.1.call-update) | async-done | bytes 2359312 | tf_op jit(solution)/shard_map/all_gather | solution.py:226
  1722.1 62.6 %all-reduce.22.cloned.1.call-done = (bf16[128,1024]{1,0:T(8,128)(2,1)}, bf16[128,1024]{1,0:T(8,128)(2,1)}, bf16[128,1024]{1,0:T(8,128)(2,1)}, bf16[128,1024]{1,0:T(8,128)(2,1)}, bf16[128,1024]{1,0:T(8,128)(2,1)}) async-done(((bf16[128,1024]{1,0:T(8,128)(2,1)}, bf16[128,1024]{1,0:T(8,128)(2,1)}, bf16[128,1024]{1,0:T(8,128)(2,1)}, bf16[128,1024]{1,0:T(8,128)(2,1)}, bf16[128,1024]{1,0:T(8,128)(2,1)}), ...) | async-done | bytes 1310736 | tf_op jit(solution)/shard_map/psum | solution.py:232
  1787.6 25.7 all-gather.59.cloned.1.call-done
  1817.0 26.1 all-gather.115.cloned.1.call-done
  1846.4 26.4 all-gather.99.cloned.1.call-done
  1876.7 25.9 all-gather.83.cloned.1.call-done
  1962.8 28.0 %all-gather.117.cloned.1.call-done = bf16[1024,1152]{1,0:T(8,128)(2,1)} async-done(((bf16[128,1152]{1,0:T(8,128)(2,1)}), bf16[1024,1152]{1,0:T(8,128)(2,1)}) %all-gather.117.cloned.1.call-update) | async-done | bytes 2359312 | tf_op jit(solution)/shard_map/all_gather | solution.py:228
  1994.1 28.2 %all-gather.101.cloned.1.call-done = bf16[1024,1152]{1,0:T(8,128)(2,1)} async-done(((bf16[128,1152]{1,0:T(8,128)(2,1)}), bf16[1024,1152]{1,0:T(8,128)(2,1)}) %all-gather.101.cloned.1.call-update) | async-done | bytes 2359312 | tf_op jit(solution)/shard_map/all_gather | solution.py:227
  2025.6 28.1 %all-gather.85.cloned.1.call-done = bf16[1024,1152]{1,0:T(8,128)(2,1)} async-done(((bf16[128,1152]{1,0:T(8,128)(2,1)}), bf16[1024,1152]{1,0:T(8,128)(2,1)}) %all-gather.85.cloned.1.call-update) | async-done | bytes 2359312 | tf_op jit(solution)/shard_map/all_gather | solution.py:226
  2057.0 474.2 %all-reduce.20.cloned.1.call-done = (bf16[3072,1024]{1,0:T(8,128)(2,1)}, bf16[3072,1024]{1,0:T(8,128)(2,1)}, bf16[128,1024]{1,0:T(8,128)(2,1)}, bf16[128,1024]{1...) async-done(((bf16[3072,1024]{1,0:T(8,128)(2,1)}, bf16[3072,1024]{1,0:T(8,128)(2,1)}, bf16[128,1024]{1,0:T(8,128)(2,1)}, ...) | async-done | bytes 13893648 | tf_op jit(solution)/shard_map/psum | solution.py:128
  2533.6 14.7 convert_add_fusion
  2557.1 23.8 all-reduce.4
  2582.2 16.4 fusion.7
  2623.5 25.6 all-gather.87.cloned.1.call-done
  2652.6 26.1 all-gather.71.cloned.1.call-done
  (437 shorter events, 530.2 us)
Async XLA Ops:
  9.2 282.5 %all-reduce.16.cloned.1.call-start = ((), (), s32[]{:S(2)}) async-start(), calls=%async_computation.6 | async-start | bytes 12582912 | tf_op jit(solution)/shard_map/psum | solution.py:116
  68.7 253.5 %all-gather.43.cloned.1.call-start = ((), (), s32[]{:S(2)}) async-start(), calls=%async_computation.7 | async-start | bytes 2654208 | tf_op jit(solution)/shard_map/all_gather | solution.py:84
  70.5 283.1 %all-gather.45.cloned.1.call-start = ((), (), s32[]{:S(2)}) async-start(), calls=%async_computation.8 | async-start | bytes 2654208 | tf_op jit(solution)/shard_map/all_gather | solution.py:85
  71.3 313.6 %all-gather.47.cloned.1.call-start = ((), (), s32[]{:S(2)}) async-start(), calls=%async_computation.9 | async-start | bytes 2654208 | tf_op jit(solution)/shard_map/all_gather | solution.py:86
  72.1 589.2 %all-reduce.18.cloned.1.call-start = ((), (), s32[]{:S(2)}) async-start(), calls=%async_computation.10 | async-start | bytes 12582912 | tf_op jit(solution)/shard_map/psum | solution.py:143
  438.3 297.4 %reduce-scatter.10.cloned.1.call-start = ((), (), s32[]{:S(2)}) async-start(), calls=%async_computation.13 | async-start | bytes 2654208 | tf_op jit(solution)/shard_map/reduce_scatter | solution.py:190
  452.5 299.9 %reduce-scatter.12.cloned.1.call-start = ((), (), s32[]{:S(2)}) async-start(), calls=%async_computation.14 | async-start | bytes 2654208 | tf_op jit(solution)/shard_map/reduce_scatter | solution.py:193
  466.2 332.1 %reduce-scatter.14.cloned.1.call-start = ((), (), s32[]{:S(2)}) async-start(), calls=%async_computation.15 | async-start | bytes 2654208 | tf_op jit(solution)/shard_map/reduce_scatter | solution.py:196
  486.5 349.7 %reduce-scatter.8.cloned.1.call-start = ((), (), s32[]{:S(2)}) async-start(), calls=%async_computation.12 | async-start | bytes 589824 | tf_op jit(solution)/shard_map/reduce_scatter | solution.py:187
  705.2 173.4 %reduce-scatter.6.cloned.1.call-start = ((), (), s32[]{:S(2)}) async-start(), calls=%async_computation.11 | async-start | bytes 1769472 | tf_op jit(solution)/shard_map/reduce_scatter | solution.py:184
  735.7 217.7 %all-gather.49.cloned.1.call-start = ((), (), s32[]{:S(2)}) async-start(), calls=%async_computation.16 | async-start | bytes 1769472 | tf_op jit(solution)/shard_map/all_gather | solution.py:224
  925.6 59.3 %all-gather.105.cloned.1.call-start = ((), (), s32[]{:S(2)}) async-start(), calls=%async_computation.44 | async-start | bytes 2654208 | tf_op jit(solution)/shard_map/all_gather | solution.py:228
  927.1 89.1 %all-gather.89.cloned.1.call-start = ((), (), s32[]{:S(2)}) async-start(), calls=%async_computation.36 | async-start | bytes 2654208 | tf_op jit(solution)/shard_map/all_gather | solution.py:227
  928.7 118.9 %all-gather.73.cloned.1.call-start = ((), (), s32[]{:S(2)}) async-start(), calls=%async_computation.28 | async-start | bytes 2654208 | tf_op jit(solution)/shard_map/all_gather | solution.py:226
  930.2 183.3 %all-reduce.26.cloned.1.call-start = ((), (), s32[]{:S(2)}) async-start(), calls=%async_computation.55 | async-start | bytes 2621440 | tf_op jit(solution)/shard_map/psum | solution.py:232
  1050.9 91.2 %all-gather.51.cloned.1.call-start = ((), (), s32[]{:S(2)}) async-start(), calls=%async_computation.17 | async-start | bytes 2359296 | tf_op jit(solution)/shard_map/all_gather | solution.py:240
  1114.1 87.5 %all-gather.91.cloned.1.call-start = ((), (), s32[]{:S(2)}) async-start(), calls=%async_computation.37 | async-start | bytes 2359296 | tf_op jit(solution)/shard_map/all_gather | solution.py:243
  1114.9 116.4 %all-gather.75.cloned.1.call-start = ((), (), s32[]{:S(2)}) async-start(), calls=%async_computation.29 | async-start | bytes 2359296 | tf_op jit(solution)/shard_map/all_gather | solution.py:242
  1115.5 145.6 %all-gather.65.cloned.1.call-start = ((), (), s32[]{:S(2)}) async-start(), calls=%async_computation.24 | async-start | bytes 2359296 | tf_op jit(solution)/shard_map/all_gather | solution.py:241
  1116.2 172.5 %all-gather.53.cloned.1.call-start = ((), (), s32[]{:S(2)}) async-start(), calls=%async_computation.18 | async-start | bytes 1769472 | tf_op jit(solution)/shard_map/all_gather | solution.py:224
  1146.0 174.3 %all-gather.109.cloned.1.call-start = ((), (), s32[]{:S(2)}) async-start(), calls=%async_computation.46 | async-start | bytes 2654208 | tf_op jit(solution)/shard_map/all_gather | solution.py:228
  1175.0 176.6 %all-gather.93.cloned.1.call-start = ((), (), s32[]{:S(2)}) async-start(), calls=%async_computation.38 | async-start | bytes 2654208 | tf_op jit(solution)/shard_map/all_gather | solution.py:227
  1205.7 177.4 %all-gather.77.cloned.1.call-start = ((), (), s32[]{:S(2)}) async-start(), calls=%async_computation.30 | async-start | bytes 2654208 | tf_op jit(solution)/shard_map/all_gather | solution.py:226
  1234.5 214.5 %all-reduce.24.cloned.1.call-start = ((), (), s32[]{:S(2)}) async-start(), calls=%async_computation.54 | async-start | bytes 2621440 | tf_op jit(solution)/shard_map/psum | solution.py:232
  1386.4 91.2 %all-gather.55.cloned.1.call-start = ((), (), s32[]{:S(2)}) async-start(), calls=%async_computation.19 | async-start | bytes 2359296 | tf_op jit(solution)/shard_map/all_gather | solution.py:240
  1449.8 87.5 %all-gather.95.cloned.1.call-start = ((), (), s32[]{:S(2)}) async-start(), calls=%async_computation.39 | async-start | bytes 2359296 | tf_op jit(solution)/shard_map/all_gather | solution.py:243
  1450.6 116.4 %all-gather.79.cloned.1.call-start = ((), (), s32[]{:S(2)}) async-start(), calls=%async_computation.31 | async-start | bytes 2359296 | tf_op jit(solution)/shard_map/all_gather | solution.py:242
  1451.1 145.6 %all-gather.67.cloned.1.call-start = ((), (), s32[]{:S(2)}) async-start(), calls=%async_computation.25 | async-start | bytes 2359296 | tf_op jit(solution)/shard_map/all_gather | solution.py:241
  1451.9 172.5 %all-gather.57.cloned.1.call-start = ((), (), s32[]{:S(2)}) async-start(), calls=%async_computation.20 | async-start | bytes 1769472 | tf_op jit(solution)/shard_map/all_gather | solution.py:224
  1481.4 174.4 %all-gather.113.cloned.1.call-start = ((), (), s32[]{:S(2)}) async-start(), calls=%async_computation.48 | async-start | bytes 2654208 | tf_op jit(solution)/shard_map/all_gather | solution.py:228
  1510.7 176.5 %all-gather.97.cloned.1.call-start = ((), (), s32[]{:S(2)}) async-start(), calls=%async_computation.40 | async-start | bytes 2654208 | tf_op jit(solution)/shard_map/all_gather | solution.py:227
  1541.2 177.6 %all-gather.81.cloned.1.call-start = ((), (), s32[]{:S(2)}) async-start(), calls=%async_computation.32 | async-start | bytes 2654208 | tf_op jit(solution)/shard_map/all_gather | solution.py:226
  1570.1 214.5 %all-reduce.22.cloned.1.call-start = ((), (), s32[]{:S(2)}) async-start(), calls=%async_computation.53 | async-start | bytes 2621440 | tf_op jit(solution)/shard_map/psum | solution.py:232
  1722.1 91.2 %all-gather.59.cloned.1.call-start = ((), (), s32[]{:S(2)}) async-start(), calls=%async_computation.21 | async-start | bytes 2359296 | tf_op jit(solution)/shard_map/all_gather | solution.py:240
  1784.7 58.4 %all-gather.115.cloned.1.call-start = ((), (), s32[]{:S(2)}) async-start(), calls=%async_computation.49 | async-start | bytes 2359296 | tf_op jit(solution)/shard_map/all_gather | solution.py:244
  1785.5 87.3 %all-gather.99.cloned.1.call-start = ((), (), s32[]{:S(2)}) async-start(), calls=%async_computation.41 | async-start | bytes 2359296 | tf_op jit(solution)/shard_map/all_gather | solution.py:243
  1786.0 116.6 %all-gather.83.cloned.1.call-start = ((), (), s32[]{:S(2)}) async-start(), calls=%async_computation.33 | async-start | bytes 2359296 | tf_op jit(solution)/shard_map/all_gather | solution.py:242
  1786.8 145.7 %all-gather.69.cloned.1.call-start = ((), (), s32[]{:S(2)}) async-start(), calls=%async_computation.26 | async-start | bytes 2359296 | tf_op jit(solution)/shard_map/all_gather | solution.py:241
  1787.5 172.5 %all-gather.61.cloned.1.call-start = ((), (), s32[]{:S(2)}) async-start(), calls=%async_computation.22 | async-start | bytes 1769472 | tf_op jit(solution)/shard_map/all_gather | solution.py:224
  1817.0 173.8 %all-gather.117.cloned.1.call-start = ((), (), s32[]{:S(2)}) async-start(), calls=%async_computation.50 | async-start | bytes 2654208 | tf_op jit(solution)/shard_map/all_gather | solution.py:228
  1846.4 176.0 %all-gather.101.cloned.1.call-start = ((), (), s32[]{:S(2)}) async-start(), calls=%async_computation.42 | async-start | bytes 2654208 | tf_op jit(solution)/shard_map/all_gather | solution.py:227
  1876.7 177.0 %all-gather.85.cloned.1.call-start = ((), (), s32[]{:S(2)}) async-start(), calls=%async_computation.34 | async-start | bytes 2654208 | tf_op jit(solution)/shard_map/all_gather | solution.py:226
  1905.8 625.5 %all-reduce.20.cloned.1.call-start = ((), (), s32[]{:S(2)}) async-start(), calls=%async_computation.52 | async-start | bytes 27787264 | tf_op jit(solution)/shard_map/psum | solution.py:128
  2057.0 541.6 %all-gather.63.cloned.1.call-start = ((), (), s32[]{:S(2)}) async-start(), calls=%async_computation.23 | async-start | bytes 2359296 | tf_op jit(solution)/shard_map/all_gather | solution.py:240
  2531.3 76.9 %all-gather.119.cloned.1.call-start = ((), (), s32[]{:S(2)}) async-start(), calls=%async_computation.51 | async-start | bytes 2359296 | tf_op jit(solution)/shard_map/all_gather | solution.py:244
  2531.9 87.3 %all-gather.103.cloned.1.call-start = ((), (), s32[]{:S(2)}) async-start(), calls=%async_computation.43 | async-start | bytes 2359296 | tf_op jit(solution)/shard_map/all_gather | solution.py:243
  2532.5 116.6 %all-gather.87.cloned.1.call-start = ((), (), s32[]{:S(2)}) async-start(), calls=%async_computation.35 | async-start | bytes 2359296 | tf_op jit(solution)/shard_map/all_gather | solution.py:242
  2533.2 145.5 %all-gather.71.cloned.1.call-start = ((), (), s32[]{:S(2)}) async-start(), calls=%async_computation.27 | async-start | bytes 2359296 | tf_op jit(solution)/shard_map/all_gather | solution.py:241
  (108 other events, 4831.9 us)
Sparse Core Ops, SparseCore 0:
  10.5 28.5 all-gather.40
  68.8 222.8 all-reduce.15
  294.2 27.9 all-gather.42
  324.5 29.0 all-gather.44
  355.8 29.0 all-gather.46
  438.4 222.8 all-reduce.17
  664.7 41.4 reduce-scatter.9
  709.9 42.4 reduce-scatter.11
  755.7 42.5 reduce-scatter.13
  802.1 34.0 reduce-scatter.7
  840.1 38.4 reduce-scatter.5
  925.7 27.6 all-gather.48
  955.9 29.0 all-gather.104
  987.2 29.0 all-gather.88
  1018.6 29.0 all-gather.72
  1051.4 62.1 all-reduce.25
  1115.3 26.8 all-gather.50
  1143.9 27.8 all-gather.106
  1173.7 27.8 all-gather.90
  1203.4 27.8 all-gather.74
  1233.2 27.8 all-gather.64
  1291.2 29.0 all-gather.108
  1322.6 29.0 all-gather.92
  1354.1 29.0 all-gather.76
  1386.9 62.1 all-reduce.23
  1450.8 26.8 all-gather.54
  1479.5 27.8 all-gather.110
  1509.4 27.8 all-gather.94
  1539.0 27.8 all-gather.78
  1568.8 27.8 all-gather.66
  1626.7 29.0 all-gather.112
  1658.2 29.0 all-gather.96
  1689.7 29.0 all-gather.80
  1722.5 62.1 all-reduce.21
  1786.4 26.8 all-gather.58
  1815.2 27.8 all-gather.114
  1844.9 27.8 all-gather.98
  1874.7 27.8 all-gather.82
  1904.5 27.8 all-gather.68
  1961.8 29.0 all-gather.116
  1993.3 29.0 all-gather.100
  2024.6 29.0 all-gather.84
  2058.6 472.5 all-reduce.19
  2533.0 26.7 all-gather.62
  2561.6 27.9 all-gather.118
  2591.3 27.8 all-gather.102
  2621.1 27.8 all-gather.86
  2650.8 27.8 all-gather.70
  (3 shorter events, 76.9 us)
where the time goes:
time: 2700 us; the launch traced here: 2690 us
  waiting for transfers between devices  2080 us (77%)
  matrix products  292 us (11%)
  other arithmetic  135 us (5%)
  blocking collectives  115 us (4%)
  local copies, waits for them, and re-layouts  45.2 us (2%)
    psum x1, waiting for transfers between devices, on_device(): lax.psum(contract_last(activated, down_full).astype(jnp.bfloat16), 'chan')  474 us
    psum x1, waiting for transfers between devices, on_device(): lax.psum(contract_last(mixer_input, out_full).astype(jnp.bfloat16), 'chan')  210 us
    psum x3, waiting for transfers between devices, on_device(): lax.psum(partial_value[0].astype(jnp.bfloat16), 'chan').astype(jnp.float32)  188 us
    psum x1, waiting for transfers between devices, on_device(): lax.psum(second_part.astype(jnp.bfloat16), 'chan').astype(jnp.float32)  175 us
    all_gather x4, waiting for transfers between devices, on_device(): lax.all_gather(states[4], 'seq', axis=0, tiled=True)  114 us
    all_gather x4, waiting for transfers between devices, on_device(): lax.all_gather(states[3], 'seq', axis=0, tiled=True)  113 us
    all_gather x4, waiting for transfers between devices, on_device(): lax.all_gather(states[2], 'seq', axis=0, tiled=True)  113 us
    dot_general x25, matrix products, contract_last(): lax.dot_general(left, right, (((1,), (1,)), ((), ())), preferred_element_...  110 us
  transfers between devices with their start and end apart: 53, of which 48 were waited for; matrix products, arithmetic and copies ran while one was open for 13% of the time, Pallas kernels for 0%

commit v1 on v0

v1 whole, which is shorter than its diff:
```python
import functools
import math

import jax
import jax.numpy as jnp
from jax import lax
from jax.experimental import pallas as pl
from jax.experimental.pallas import tpu as pltpu
from jax.sharding import PartitionSpec as P

D = 1024
FF = 4608
NS_ITERS = 4
STEP = 10


NORM_EPS = 1e-05
QUINTIC_FIRST = 3.4445
QUINTIC_SECOND = -4.775
QUINTIC_THIRD = 2.0315
MOMENTUM_DECAY = 0.95
FIRST_DECAY = 0.9
SECOND_DECAY = 0.999
ADAM_EPS = 1e-08
ADAM_RATE = 0.4
WEIGHT_DECAY = 0.01
ORTHO_EPS = 1e-07

MESH = pl.DeviceIdType.MESH
BF16 = jnp.bfloat16
F32 = jnp.float32

PIECES = 32
PER_CHAN = 8
PIECE = FF // PIECES
LANES = 128
TILES = FF // 4 // LANES
UNIT = LANES // PER_CHAN
SMALL_PIECE = 4 * D // PIECES
IN_PIECES = 6


def remote(src, dst, send, recv, **place):
    return pltpu.make_async_remote_copy(
        src_ref=src, dst_ref=dst, send_sem=send, recv_sem=recv, device_id=place, device_id_type=MESH
    )


def flip(index, bit):
    step = 1 << bit
    return index + step * (1 - 2 * lax.rem(lax.div(index, step), 2))


def flips(index, bits):
    found = [index]
    for bit in bits:
        found = found + [flip(one, bit) for one in found]
    return found


def greet(places):
    barrier = pltpu.get_barrier_semaphore()
    for place in places:
        pl.semaphore_signal(barrier, inc=1, device_id=place, device_id_type=MESH)
    pl.semaphore_wait(barrier, len(places))


def high_bits(bits, half):
    order = list(range(1, bits))
    return order if half == 0 else order[::-1]


def call(kernel, outs, in_spaces, out_spaces, scratch, ident, *args, vmem=48):
    return pl.pallas_call(
        kernel,
        out_shape=outs,
        in_specs=[pl.BlockSpec(memory_space=space) for space in in_spaces],
        out_specs=jax.tree.map(lambda space: pl.BlockSpec(memory_space=space), out_spaces),
        scratch_shapes=scratch,
        compiler_params=pltpu.CompilerParams(
            collective_id=ident, has_side_effects=True, vmem_limit_bytes=vmem * 1024 * 1024
        ),
    )(*args)


def holder(r, c, seqs):
    at = lax.rem(r + PIECES * seqs - PER_CHAN * c, seqs)
    return at, at < PER_CHAN, lax.div(PER_CHAN * c + at, seqs)


class Homeward:
    def __init__(self, seqs, chans, held, out, between, sems):
        self.seqs, self.chans, self.held, self.out, self.between = seqs, chans, held, out, between
        self.own_sem, self.stay_sem, self.a_send, self.a_recv, self.b_send, self.b_recv = sems
        self.r, self.c = lax.axis_index("seq"), lax.axis_index("chan")
        self.at_out, self.has, self.place = holder(self.r, self.c, seqs)

    def target(self, at):
        return lax.div(self.r + self.seqs * at, PER_CHAN)

    def dropping(self, at):
        return remote(
            self.held.at[at], self.between.at[self.c], self.a_send.at[at], self.a_recv.at[self.c],
            chan=self.target(at),
        )

    def keeping(self, at):
        return pltpu.make_async_copy(self.held.at[at], self.between.at[self.c], self.own_sem.at[0])

    def spreading(self, m, r_to):
        return remote(
            self.between.at[m, r_to], self.out.at[m, self.at_out],
            self.b_send.at[m, r_to], self.b_recv.at[m, self.at_out], seq=r_to,
        )

    def staying(self, m):
        return pltpu.make_async_copy(
            self.between.at[m, self.r], self.out.at[m, self.at_out], self.stay_sem.at[m]
        )

    def drop(self, at):
        @pl.when(self.target(at) != self.c)
        def _():
            self.dropping(at).start()

        @pl.when(self.target(at) == self.c)
        def _():
            self.keeping(at).start()

    def spread(self):
        @pl.when(self.has)
        def _():
            for off in (0, 1, 3, 2):
                m = lax.rem(self.c + off, self.chans)
                if off == 0:
                    self.keeping(0).wait()
                else:
                    remote(
                        self.held.at[0], self.between.at[m], self.a_send.at[0], self.a_recv.at[m], chan=m
                    ).wait_recv()
                for step in range(1, self.seqs):
                    self.spreading(m, lax.rem(self.r + step, self.seqs)).start()
                self.staying(m).start()

    def finish(self):
        @pl.when(self.has)
        def _():
            for m in range(self.chans):
                self.staying(m).wait()

        for piece in range(PER_CHAN):
            r_from = lax.rem(PER_CHAN * self.c + piece, self.seqs)

            @pl.when(r_from != self.r)
            def _():
                for m in range(self.chans):
                    remote(
                        self.between.at[m, self.r], self.out.at[m, piece],
                        self.b_send.at[m, self.r], self.b_recv.at[m, piece], seq=r_from,
                    ).wait_recv()

        for at in range(PIECES // self.seqs):

            @pl.when(self.target(at) != self.c)
            def _():
                self.dropping(at).wait_send()

        @pl.when(self.has)
        def _():
            for m in range(self.chans):
                for step in range(1, self.seqs):
                    self.spreading(m, lax.rem(self.r + step, self.seqs)).wait_send()

    @staticmethod
    def semaphores(seqs, chans):
        dma = pltpu.SemaphoreType.DMA
        return [
            dma((1,)), dma((chans,)), dma((PIECES // seqs,)), dma((chans,)),
            dma((chans, seqs)), dma((chans, PER_CHAN)),
        ]


class Relay:
    def __init__(self, chans, own, blocks, sems):
        self.chans, self.own, self.blocks = chans, own, blocks
        self.own_sem, self.send, self.recv = sems
        self.c = lax.axis_index("chan")

    def keeping(self):
        return pltpu.make_async_copy(self.own, self.blocks.at[self.c], self.own_sem.at[0])

    def copies(self, hop):
        c = self.c
        for side, block, sends in (
            (0, c - hop, (c < self.chans - 1) & (c >= hop)),
            (1, c + hop, (c > 0) & (c + hop < self.chans)),
        ):
            source = self.own if hop == 0 else self.blocks.at[block]
            yield sends, remote(
                source, self.blocks.at[block], self.send.at[side, hop], self.recv.at[side, hop],
                chan=c + 1 - 2 * side,
            )

    def await_hop(self, hop):
        c = self.c
        for side, block, comes in ((0, c - 1 - hop, c > hop), (1, c + 1 + hop, c + 1 + hop < self.chans)):

            @pl.when(comes)
            def _():
                remote(
                    self.own, self.blocks.at[block], self.send.at[side, hop], self.recv.at[side, hop],
                    chan=c - 1 + 2 * side,
                ).wait_recv()

    def step(self, hop):
        if hop == 0:
            self.keeping().start()
        else:
            self.await_hop(hop - 1)
        for sends, copy in self.copies(hop):

            @pl.when(sends)
            def _():
                copy.start()

    def finish(self):
        self.await_hop(self.chans - 2)
        self.keeping().wait()
        for hop in range(self.chans - 1):
            for sends, copy in self.copies(hop):

                @pl.when(sends)
                def _():
                    copy.wait_send()

    @staticmethod
    def semaphores(chans):
        dma = pltpu.SemaphoreType.DMA
        return [dma((1,)), dma((2, chans - 1)), dma((2, chans - 1))]


def dot(left, right):
    return jnp.dot(left, right, preferred_element_type=F32)


def contract_last(left, right):
    return lax.dot_general(left, right, (((1,), (1,)), ((), ())), preferred_element_type=F32)


def contract_first(left, right):
    return lax.dot_general(left, right, (((0,), (0,)), ((), ())), preferred_element_type=F32)


def ortho_kernel(
    seqs, chans, grad, moment, input_grad, grad_home, ortho_home, input_blocks,
    out, cut_grad, cut_ortho, between_grad, between_ortho,
    part, own, swapped, paired, parts, sums, gram, poly, half_way,
    x_send, x_recv, s_send, s_recv, g_send, g_recv, f_send, f_recv, *home_sems
):
    r, c = lax.axis_index("seq"), lax.axis_index("chan")
    core, h = lax.rem(r, 2), lax.div(r, 2)
    other = flip(r, 0)
    count, half, block = seqs // 2, D // 2, D // seqs
    tile = min(256, half)
    peers = [lax.rem(h + off, count) for off in range(1, count)]
    greet(
        [{"seq": lax.rem(r + off, seqs)} for off in range(1, seqs)]
        + [{"chan": lax.rem(c + off, chans)} for off in range(1, chans)]
    )
    home_grad = Homeward(seqs, chans, cut_grad, grad_home, between_grad, home_sems[:6])
    home_ortho = Homeward(seqs, chans, cut_ortho, ortho_home, between_ortho, home_sems[6:12])
    relay = Relay(chans, input_grad, input_blocks, home_sems[12:])
    columns = out.shape[0]
    slab = PIECE

    @pl.loop(0, columns // slab)
    def _(at):
        here = pl.ds(pl.multiple_of(at * slab, slab), slab)
        out[here] = (MOMENTUM_DECAY * moment[here].astype(F32) + grad[here].astype(F32)).astype(BF16)
        for to in range(seqs):
            cut_grad[at, to] = grad[here, to * block : (to + 1) * block]

    for at in range(columns // slab):
        home_grad.drop(at)
    relay.step(0)

    apart = c == chans - 1

    def kind(pair):
        return jnp.where(lax.rem(pair, 4) == 3, 1, 0)

    mine = kind(h)
    own_first = pl.multiple_of(core * half, half)
    other_first = pl.multiple_of((1 - core) * half, half)

    def block_at(pair, which):
        return pl.ds(pl.multiple_of(which * half + pair * block, block), block)

    def exchange():
        return remote(part, swapped, x_send, x_recv, seq=other)

    def scatter(peer):
        return remote(
            paired.at[peer], parts.at[h], s_send.at[peer], s_recv.at[h], seq=2 * peer + core
        )

    def scatter_in(peer):
        return remote(
            paired.at[peer], parts.at[peer], s_send.at[peer], s_recv.at[peer], seq=2 * peer + core
        )

    def share(peer):
        return remote(
            sums.at[kind(peer)], gram.at[block_at(h, core)], g_send.at[peer], g_recv.at[h],
            seq=2 * peer + core,
        )

    def share_in(peer):
        return remote(
            sums.at[0], gram.at[block_at(peer, core)], g_send.at[peer], g_recv.at[peer],
            seq=2 * peer + core,
        )

    def forward(pair):
        return remote(
            gram.at[block_at(pair, core)], gram.at[block_at(pair, core)],
            f_send.at[pair], f_recv.at[pair], seq=other,
        )

    def forward_in(pair):
        return remote(
            gram.at[block_at(pair, 1 - core)], gram.at[block_at(pair, 1 - core)],
            f_send.at[pair], f_recv.at[pair], seq=other,
        )

    for turn in range(NS_ITERS // 2):

        @pl.loop(0, half // tile)
        def _(at):
            here = pl.ds(pl.multiple_of(at * tile, tile), tile)
            there = pl.ds(pl.multiple_of(other_first + at * tile, tile), tile)
            part[here] = contract_first(out[:, there], out[...]).astype(BF16)

        exchange().start()

        @pl.loop(0, half // tile)
        def _(at):
            here = pl.ds(pl.multiple_of(at * tile, tile), tile)
            there = pl.ds(pl.multiple_of(own_first + at * tile, tile), tile)
            own[here] = contract_first(out[:, there], out[...])

        exchange().wait()

        @pl.loop(0, count)
        def _(at):
            here = pl.ds(pl.multiple_of(at * block, block), block)
            paired[at] = (own[here] + swapped[here].astype(F32)).astype(BF16)

        for peer in peers:
            scatter(peer).start()
        parts[h] = paired[h]
        for peer in peers:
            scatter_in(peer).wait_recv()
        groups = [jnp.zeros((block, D), F32), jnp.zeros((block, D), F32)]
        for pair in range(count):
            groups[int(pair % 4 == 3)] += parts[pair].astype(F32)
        both = groups[0] + groups[1]
        sums[0] = jnp.where(apart, groups[0], both).astype(BF16)
        sums[1] = jnp.where(apart, groups[1], both).astype(BF16)
        for peer in peers:
            share(peer).start()
        gram[block_at(h, core)] = sums[mine]
        forward(h).start()
        for peer in peers:
            share_in(peer).wait_recv()
            forward(peer).start()
        for pair in [h] + peers:
            forward_in(pair).wait_recv()
        for peer in peers:
            scatter(peer).wait_send()
            share(peer).wait_send()
        for pair in [h] + peers:
            forward(pair).wait_send()
        if turn == 1:
            relay.step(2)

        scale = jnp.ones((1, 1), F32)
        if turn == 0:
            trace = jnp.zeros((1, 1), F32)
            for at in range(D // 128):
                square = gram[at * 128 : (at + 1) * 128, at * 128 : (at + 1) * 128].astype(F32)
                row = lax.broadcasted_iota(jnp.int32, square.shape, 0)
                column = lax.broadcasted_iota(jnp.int32, square.shape, 1)
                trace += jnp.sum(jnp.where(row == column, square, 0.0), keepdims=True)
            scale = 1.0 / (jnp.sqrt(trace) + ORTHO_EPS)

            @pl.loop(0, D // tile)
            def _(at):
                here = pl.ds(pl.multiple_of(at * tile, tile), tile)
                gram[here] = (gram[here].astype(F32) * scale * scale).astype(BF16)

        def each_tile(work):
            @pl.loop(0, D // tile)
            def _(at):
                work(pl.ds(pl.multiple_of(at * tile, tile), tile))

        def polynomial(values, whole):
            return (
                QUINTIC_SECOND * values.astype(F32) + QUINTIC_THIRD * dot(values, whole[...])
            ).astype(BF16)

        def first_poly(here):
            poly[here] = polynomial(gram[here], gram)

        def halfway(here):
            half_way[here] = (
                QUINTIC_FIRST * gram[here].astype(F32) + dot(poly[here], gram[...])
            ).astype(BF16)

        def next_gram(here):
            gram[here] = (
                QUINTIC_FIRST * half_way[here].astype(F32) + dot(half_way[here], poly[...])
            ).astype(BF16)

        def second_poly(here):
            half_way[here] = polynomial(gram[here], gram)

        for work in (first_poly, halfway, next_gram, second_poly):
            each_tile(work)

        @pl.loop(0, columns // slab)
        def _(at):
            here = pl.ds(pl.multiple_of(at * slab, slab), slab)
            new = QUINTIC_FIRST * out[here].astype(F32) + dot(out[here], poly[...])
            if turn == 0:
                new = new * scale
            new = QUINTIC_FIRST * new + dot(new.astype(BF16), half_way[...])
            if turn < NS_ITERS // 2 - 1:
                out[here] = new.astype(BF16)
            else:
                for to in range(seqs):
                    cut_ortho[at, to] = new[:, to * block : (to + 1) * block].astype(BF16)
                home_ortho.drop(at)

        if turn == 0:
            home_grad.spread()
            relay.step(1)

    home_ortho.spread()
    home_grad.finish()
    relay.finish()
    home_ortho.finish()


def orthogonalize(seqs, chans, grad, moment, input_grad):
    dma = pltpu.SemaphoreType.DMA
    count, block, held = seqs // 2, D // seqs, PIECES // seqs
    return call(
        functools.partial(ortho_kernel, seqs, chans),
        [jax.ShapeDtypeStruct((chans, PER_CHAN, PIECE, block), BF16)] * 2
        + [jax.ShapeDtypeStruct((chans,) + input_grad.shape, BF16)],
        [pltpu.VMEM] * 2 + [pl.ANY],
        [pl.ANY] * 3,
        [
            pltpu.VMEM(grad.shape, BF16),
            pltpu.VMEM((held, seqs, PIECE, block), BF16),
            pltpu.VMEM((held, seqs, PIECE, block), BF16),
            pltpu.VMEM((chans, seqs, PIECE, block), BF16),
            pltpu.VMEM((chans, seqs, PIECE, block), BF16),
            pltpu.VMEM((D // 2, D), BF16),
            pltpu.VMEM((D // 2, D), F32),
            pltpu.VMEM((D // 2, D), BF16),
            pltpu.VMEM((count, block, D), BF16),
            pltpu.VMEM((count, block, D), BF16),
            pltpu.VMEM((2, block, D), BF16),
            pltpu.VMEM((D, D), BF16),
            pltpu.VMEM((D, D), BF16),
            pltpu.VMEM((D, D), BF16),
            dma(()),
            dma(()),
        ]
        + [dma((count,))] * 6
        + Homeward.semaphores(seqs, chans) * 2
        + Relay.semaphores(chans),
        2,
        grad,
        moment,
        input_grad,
    )


HEAD = 8


def own_rows(values, seqs_held):
    length = values.shape[0] // seqs_held
    return [values[s * length + HEAD : (s + 1) * length] for s in range(seqs_held)]


def row_scale(values):
    return lax.rsqrt(jnp.mean(values * values, axis=1, keepdims=True) + NORM_EPS)


def filtering(gated, taps, keep_one, keep_two):
    back_one, back_two = pltpu.roll(gated, 1, 0), pltpu.roll(gated, 2, 0)
    return taps[2:3] * gated + taps[1:2] * keep_one * back_one + taps[0:1] * keep_two * back_two


def forward_kernel(seqs, chans, held, *refs):
    forward_work(seqs, chans, held, refs[:5], refs[5:10], *refs[10:])


def forward_work(
    seqs, chans, held,
    weights, moments, own_taps, token_source, cotangent_source, keeps, gains,
    in_full, out_full, ffn_full, taps_all, held_out, between, streams, ffn_g,
    tokens, cotangent, residual, second_grad, block_out,
    in_shard, out_shard, ffn_shard, taps, packed, shelf, shelf_sem,
    u, u_own, halo, row_sem, halo_sem, halo_send, halo_recv, normed, mixed, stream, x, x_own, ffn_out, act, gate_low, up_low, in_v, out_v, taps_v, w_v, grad_v,
    own_sem, z_send, z_recv, b_send, b_recv, c_send, c_recv,
    t_own, t_send, t_recv, p_own, ps_send, ps_recv, pl_send, pl_recv,
    mix_sem, taps_sem, stream_sem, load_sem, grad_sem,
):
    bits = seqs.bit_length() - 1
    r, c = lax.axis_index("seq"), lax.axis_index("chan")
    last = TILES + 1
    greet(
        [{"chan": lax.rem(c + off, chans)} for off in range(1, chans)]
        + [{"seq": lax.rem(r + off, seqs)} for off in range(1, seqs)]
    )

    def shard(k):
        if isinstance(k, int) and k < 2:
            return (in_shard, out_shard)[k]
        return ffn_shard.at[k - 2]

    def full(k, part, block):
        if isinstance(k, int) and k < 2:
            return (in_full, out_full)[k].at[part, block]
        return ffn_full.at[k - 2, part, block]

    def own(k):
        return pltpu.make_async_copy(shard(k), full(k, c, r), own_sem.at[k])

    def along_chan(k, off, incoming):
        source = lax.rem(c + chans - off, chans) if incoming else c
        return remote(
            shard(k), full(k, source, r), z_send.at[k, off - 1], z_recv.at[k, off - 1],
            chan=lax.rem(c + off, chans),
        )

    def across(k, half, step, incoming):
        order = high_bits(bits, half)
        bit, done = order[step], order[:step]
        base = flip(r, bit) if incoming else r
        part = pl.ds(half * (chans // 2), chans // 2)
        first = (1 << step) - 1
        return [
            remote(
                full(k, part, block), full(k, part, block),
                b_send.at[k, half, first + at], b_recv.at[k, half, first + at], seq=flip(r, bit),
            )
            for at, block in enumerate(flips(base, done))
        ]

    def core(k, incoming):
        base = flip(r, 0) if incoming else r
        return [
            remote(
                full(k, slice(None), block), full(k, slice(None), block),
                c_send.at[k, at], c_recv.at[k, at], seq=flip(r, 0),
            )
            for at, block in enumerate(flips(base, range(1, bits)))
        ]

    def start_chan(k):
        own(k).start()
        for off in (2, 1, 3):
            along_chan(k, off, False).start()

    def first_level(k):
        own(k).wait()
        for off in range(1, chans):
            along_chan(k, off, True).wait_recv()
        for half in range(2):
            for copy in across(k, half, 0, False):
                copy.start()

    def next_level(k, level):
        for half in range(2):
            for copy in across(k, half, level - 1, True):
                copy.wait_recv()
            for copy in across(k, half, level, False):
                copy.start()

    def to_core(k):
        for half in range(2):
            for copy in across(k, half, bits - 2, True):
                copy.wait_recv()
        for copy in core(k, False):
            copy.start()

    def arrived(k):
        for copy in core(k, True):
            copy.wait_recv()

    def sent(k):
        for off in range(1, chans):
            along_chan(k, off, False).wait_send()
        for half in range(2):
            for step in range(bits - 1):
                for copy in across(k, half, step, False):
                    copy.wait_send()
        for copy in core(k, False):
            copy.wait_send()

    def taps_copy(off, incoming):
        source = lax.rem(c + chans - off, chans) if incoming else c
        return remote(
            taps, taps_all.at[source], t_send.at[off - 1], t_recv.at[off - 1],
            chan=lax.rem(c + off, chans),
        )

    _, has, place = holder(r, c, seqs)

    def spread(piece, r_to):
        return remote(
            packed.at[:, piece], between.at[:, r], ps_send.at[piece], ps_recv.at[r], seq=r_to
        )

    def lift(m):
        return remote(between.at[m], held_out.at[place], pl_send.at[m], pl_recv.at[place], chan=m)

    def pieces_start():
        for piece in range(PER_CHAN):
            r_to = lax.rem(PER_CHAN * c + piece, seqs)

            @pl.when(r_to != r)
            def _():
                spread(piece, r_to).start()

            @pl.when(r_to == r)
            def _():
                pltpu.make_async_copy(packed.at[:, piece], between.at[:, r], p_own.at[0]).start()

    def pieces_lift():
        @pl.when(has)
        def _():
            pltpu.make_async_copy(packed.at[:, 0], between.at[:, r], p_own.at[0]).wait()
            for off in range(1, seqs):
                r_from = lax.rem(r + off, seqs)
                remote(
                    packed.at[:, 0], between.at[:, r_from], ps_send.at[0], ps_recv.at[r_from], seq=r_from
                ).wait_recv()
            for m in range(chans):

                @pl.when(m != c)
                def _():
                    lift(m).start()

                @pl.when(m == c)
                def _():
                    copy = pltpu.make_async_copy(between.at[m], held_out.at[place], p_own.at[1])
                    copy.start()
                    copy.wait()

    def pieces_finish():
        for at in range(PIECES // seqs):
            c_from = lax.div(r + seqs * at, PER_CHAN)

            @pl.when(c_from != c)
            def _():
                remote(
                    between.at[0], held_out.at[at], pl_send.at[0], pl_recv.at[at], chan=c_from
                ).wait_recv()

        for piece in range(PER_CHAN):
            r_to = lax.rem(PER_CHAN * c + piece, seqs)

            @pl.when(r_to != r)
            def _():
                spread(piece, r_to).wait_send()

        @pl.when(has)
        def _():
            for m in range(chans):

                @pl.when(m != c)
                def _():
                    lift(m).wait_send()

    rows, width = tokens.shape
    part = out_full.shape[-1]
    tile = rows // 3
    per_tile = held // 3
    size = rows // held - HEAD
    tiles = [pl.ds(at * tile, tile) for at in range(3)]

    def mix_loads(j):
        slot = lax.rem(j, 2)
        return [
            pltpu.make_async_copy(in_full.at[j], in_v.at[slot], mix_sem.at[slot, 0]),
            pltpu.make_async_copy(out_full.at[j], out_v.at[slot], mix_sem.at[slot, 1]),
        ]

    def stream_out(j):
        return pltpu.make_async_copy(stream, streams.at[j], stream_sem)

    local_rows = token_source.shape[1]
    before_at = pl.multiple_of(lax.rem(c + chans - 1, chans) * size + size - HEAD, HEAD)
    after_at = pl.multiple_of(lax.rem(c + 1, chans) * size, HEAD)
    halos = [
        (token_source, before_at, c == 0, r > 0, r < seqs - 1, 1),
        (token_source, after_at, c == chans - 1, r < seqs - 1, r > 0, -1),
        (cotangent_source, after_at, c == chans - 1, r < seqs - 1, r > 0, -1),
    ]

    def row_copies():
        return [
            pltpu.make_async_copy(
                source.at[s, pl.ds(pl.multiple_of(c * size, size), size)],
                rows_to.at[pl.ds(s * (size + HEAD) + HEAD, size)],
                row_sem.at[n, s],
            )
            for n, (source, rows_to) in enumerate(
                ((token_source, tokens), (cotangent_source, cotangent))
            )
            for s in range(held)
        ]

    def halo_local(n):
        source, at, _, _, _, _ = halos[n]
        return pltpu.make_async_copy(source.at[:, pl.ds(at, HEAD)], halo.at[n], halo_sem.at[n])

    def halo_remote(n):
        source, at, _, _, _, step = halos[n]
        return remote(
            source.at[:, pl.ds(at, HEAD)], halo.at[n], halo_send.at[n], halo_recv.at[n], seq=r + step
        )

    def rows_start():
        for copy in row_copies():
            copy.start()
        for n, (_, _, edge, takes, gives, _) in enumerate(halos):

            @pl.when(jnp.logical_not(edge))
            def _():
                halo_local(n).start()

            @pl.when(edge & gives)
            def _():
                halo_remote(n).start()

            @pl.when(edge & jnp.logical_not(takes))
            def _():
                halo[n] = jnp.zeros(halo.shape[1:], F32)

    def rows_finish():
        for copy in row_copies():
            copy.wait()
        for n, (_, _, edge, takes, gives, _) in enumerate(halos):

            @pl.when(jnp.logical_not(edge))
            def _():
                halo_local(n).wait()

            @pl.when(edge & takes)
            def _():
                halo_remote(n).wait_recv()

            @pl.when(edge & gives)
            def _():
                halo_remote(n).wait_send()

        row = lax.broadcasted_iota(jnp.int32, (HEAD, width), 0)
        for s in range(held):
            head = pl.ds(s * (size + HEAD), HEAD)
            earlier = (s - 1) % held
            tokens[head] = jnp.where(row < 2, halo[1, earlier], halo[0, s])
            cotangent[head] = jnp.where(row < 2, halo[2, earlier], 0.0)
        for at, here in enumerate(tiles):
            values = cotangent[here]
            u[here] = values.astype(BF16)
            for s, one in enumerate(own_rows(values, per_tile)):
                u_own[pl.ds((at * per_tile + s) * size, size)] = one.astype(BF16)

    def mix_prepare():
        rows_finish()
        for here in tiles:
            values = tokens[here]
            normed[here] = (values * row_scale(values) * gains[0:1]).astype(BF16)
            residual[here] = values

    def mix():
        for copy in mix_loads(0):
            copy.start()
        copy = pltpu.make_async_copy(taps_all, taps_v, taps_sem)
        copy.start()
        copy.wait()

        @pl.loop(0, chans)
        def _(j):
            slot = lax.rem(j, 2)
            for copy in mix_loads(j):
                copy.wait()

            @pl.when(j + 1 < chans)
            def _():
                for copy in mix_loads(j + 1):
                    copy.start()

            @pl.when(j > 0)
            def _():
                stream_out(j - 1).wait()

            in_w = in_v[slot].reshape(width, 3 * part)
            out_w = out_v[slot].reshape(width, part)
            for here in tiles:
                stream[here] = dot(normed[here], in_w)
            filters = taps_v[j]
            gated = stream[:, 0:part] * stream[:, 2 * part :]
            filtered = filtering(gated, filters, keeps[:, 0:1], keeps[:, 1:2])
            mixed[...] = (stream[:, part : 2 * part] * filtered).astype(BF16)
            stream_out(j).start()
            for here in tiles:
                residual[here] += contract_last(mixed[here], out_w)

        for at, here in enumerate(tiles):
            values = residual[here]
            new = values * row_scale(values) * gains[1:2]
            x[here] = new.astype(BF16)
            for s, one in enumerate(own_rows(new, per_tile)):
                x_own[pl.ds((at * per_tile + s) * size, size)] = one.astype(BF16)
            ffn_out[here] = jnp.zeros((tile, width), F32)
            second_grad[here] = jnp.zeros((tile, width), F32)
        stream_out(chans - 1).wait()

    def loads(t):
        slot = lax.rem(t, 2)
        return [
            pltpu.make_async_copy(
                ffn_full.at[t, j, :, m],
                w_v.at[slot, m, :, :, pl.ds(j * LANES, LANES)],
                load_sem.at[slot, m, j],
            )
            for m in range(3)
            for j in range(chans)
        ]

    def grads_out(t):
        slot = lax.rem(t, 2)
        return [
            pltpu.make_async_copy(grad_v.at[slot, m], ffn_g.at[m, :, t], grad_sem.at[slot, m])
            for m in range(3)
        ]

    def feed_forward(t):
        slot = lax.rem(t, 2)
        for copy in loads(t):
            copy.wait()

        @pl.when(t >= 2)
        def _():
            for copy in grads_out(t - 2):
                copy.wait()

        wg, wu, wd = (w_v[slot, m].reshape(width, chans * LANES) for m in range(3))
        for at, here in enumerate(tiles):
            gate = dot(x[here], wg)
            up = dot(x[here], wu)
            grad = dot(u[here], wd)
            sigmoid = jax.nn.sigmoid(gate)
            silu = gate * sigmoid
            new_act = silu * up
            new_gate = grad * up * sigmoid * (1.0 + gate * (1.0 - sigmoid))
            new_up = grad * silu
            for ref, values in ((act, new_act), (gate_low, new_gate), (up_low, new_up)):
                for s, one in enumerate(own_rows(values, per_tile)):
                    ref[pl.ds((at * per_tile + s) * size, size)] = one.astype(BF16)
            ffn_out[here] += contract_last(new_act.astype(BF16), wd)
            second_grad[here] += contract_last(new_gate.astype(BF16), wg) + contract_last(
                new_up.astype(BF16), wu
            )
        for m, (low, right) in enumerate(((gate_low, x_own), (up_low, x_own), (act, u_own))):
            grad_v[slot, m] = (
                contract_first(low[...], right[...]).astype(BF16).reshape(PIECES, UNIT, width)
            )
        for copy in grads_out(t):
            copy.start()

    def shelf_copies(group, n):
        slot = n % 2
        if n % 4 == 0:
            part_of = [(group[0].at[k], k) for k in range(3)] + [(group[1], 3)]
            return [
                pltpu.make_async_copy(
                    source, shelf.at[slot, :, pl.ds(k * part, part)], shelf_sem.at[slot, k]
                )
                for source, k in part_of
            ]
        return [pltpu.make_async_copy(group[n % 4 + 1], shelf.at[slot], shelf_sem.at[slot, 0])]

    def shelves(n):
        return shelf_copies(weights if n < 4 else moments, n)

    for copy in shelves(0):
        copy.start()
    taps[...] = jnp.zeros_like(taps)
    taps[0:3] = own_taps[...]
    rows_start()
    for n in range(8):
        if n < 7:
            for copy in shelves(n + 1):
                copy.start()
        for copy in shelves(n):
            copy.wait()
        slot, m = n % 2, n % 4 - 1
        if n == 0:
            in_shard[...] = shelf[slot, :, : 3 * part].astype(BF16)
            out_shard[...] = shelf[slot, :, 3 * part : 4 * part].astype(BF16)
            start_chan(0)
            start_chan(1)
        elif n < 4:
            for t in range(TILES):
                ffn_shard[t, m] = shelf[slot, :, t * LANES : (t + 1) * LANES].astype(BF16)
        elif n == 4:
            packed[3] = jnp.zeros(packed.shape[1:], BF16)
            for q in range(PER_CHAN):
                block = shelf[slot, :, q * SMALL_PIECE : (q + 1) * SMALL_PIECE]
                packed[3, q, 0:SMALL_PIECE] = block.T.astype(BF16)
        else:
            for t in range(TILES):
                block = shelf[slot, :, t * LANES : (t + 1) * LANES].T.astype(BF16)
                packed[m, :, t * UNIT : (t + 1) * UNIT] = block.reshape(PER_CHAN, UNIT, -1)
    pieces_start()
    taps_own = pltpu.make_async_copy(taps, taps_all.at[c], t_own)
    taps_own.start()
    for off in range(1, chans):
        taps_copy(off, False).start()
    mix_prepare()

    for tick in range(bits + 2):
        start_chan(tick + 2)
        first_level(tick)
        for level in range(1, bits - 1):
            if tick >= level:
                next_level(tick - level, level)
        if tick >= bits - 1:
            to_core(tick - bits + 1)
        if tick >= bits:
            arrived(tick - bits)
        if tick == 1:
            pieces_lift()
    taps_own.wait()
    for off in range(1, chans):
        taps_copy(off, True).wait_recv()
    mix()

    @pl.loop(bits + 2, last + bits + 2)
    def _(tick):
        @pl.when(tick + 2 <= last)
        def _():
            start_chan(tick + 2)

        @pl.when(tick <= last)
        def _():
            first_level(tick)

        for level in range(1, bits - 1):

            @pl.when(tick - level <= last)
            def _():
                next_level(tick - level, level)

        @pl.when(tick - bits + 1 <= last)
        def _():
            to_core(tick - bits + 1)

        @pl.when(tick - bits <= last)
        def _():
            arrived(tick - bits)
            for copy in loads(tick - bits - 2):
                copy.start()

        @pl.when(tick - bits - 3 >= 0)
        def _():
            feed_forward(tick - bits - 3)

    for s in range(held):
        here = pl.ds(s * (size + HEAD) + HEAD, size)
        block_out[pl.ds(s * size, size)] = (residual[here] + ffn_out[here]).astype(BF16)
    for t in (TILES - 2, TILES - 1):
        for copy in grads_out(t):
            copy.wait()
    pieces_finish()
    for off in range(1, chans):
        taps_copy(off, False).wait_send()
    sent(0)
    sent(1)

    @pl.loop(2, last + 1)
    def _(k):
        sent(k)


def forward_pass(seqs, chans, weights, moments, taps, tokens, cotangent, keeps, gains):
    held, local_rows, width = tokens.shape
    block, part = weights[1].shape
    own_count, hidden = held * local_rows // chans, chans * LANES
    rows = own_count + held * HEAD
    tail = (PIECE, block)
    shape = jax.ShapeDtypeStruct
    outs = [
        shape((chans, seqs, block, 3 * part), BF16),
        shape((chans, seqs, block, part), BF16),
        shape((TILES, chans, seqs, 3, block, LANES), BF16),
        shape((chans, 8, part), F32),
        shape((PIECES // seqs, seqs) + tail, BF16),
        shape((chans, seqs) + tail, BF16),
        shape((chans, rows, 3 * part), F32),
    ]
    outs.append(shape((3, PIECES, TILES, UNIT, width), BF16))
    outs += [shape((rows, width), F32)] * 4 + [shape((own_count, width), BF16)]
    dma = pltpu.SemaphoreType.DMA
    count = TILES + 2
    vmem = pltpu.VMEM
    found = call(
        functools.partial(forward_kernel, seqs, chans, held),
        outs,
        [pl.ANY] * 10 + [vmem] + [pl.ANY] * 2 + [vmem] * 2,
        [pl.ANY] * 8 + [vmem] * 5,
        [
            vmem((block, 3 * part), BF16),
            vmem((block, part), BF16),
            vmem((TILES, 3, block, LANES), BF16),
            vmem((8, part), F32),
            vmem((chans, PER_CHAN) + tail, BF16),
            vmem((2, block, TILES * LANES), F32),
            dma((2, 4)),
            vmem((rows, width), BF16),
            vmem((own_count, width), BF16),
            vmem((3, held, HEAD, width), F32),
            dma((2, held)),
            dma((3,)),
            dma((3,)),
            dma((3,)),
            vmem((rows, width), BF16),
            vmem((rows, part), BF16),
            vmem((rows, 3 * part), F32),
            vmem((rows, width), BF16),
            vmem((own_count, width), BF16),
            vmem((rows, width), F32),
            vmem((own_count, hidden), BF16),
            vmem((own_count, hidden), BF16),
            vmem((own_count, hidden), BF16),
            vmem((2, seqs, block, 3 * part), BF16),
            vmem((2, seqs, block, part), BF16),
            vmem((chans, 8, part), F32),
            vmem((2, 3, seqs, block, hidden), BF16),
            vmem((2, 3, PIECES, UNIT, width), BF16),
            dma((count,)),
            dma((count, chans - 1)),
            dma((count, chans - 1)),
            dma((count, 2, seqs // 2 - 1)),
            dma((count, 2, seqs // 2 - 1)),
            dma((count, seqs // 2)),
            dma((count, seqs // 2)),
            dma(()),
            dma((chans - 1,)),
            dma((chans - 1,)),
            dma((2,)),
            dma((PER_CHAN,)),
            dma((seqs,)),
            dma((chans,)),
            dma((PIECES // seqs,)),
            dma((2, 2)),
            dma(()),
            dma(()),
            dma((2, 3, chans)),
            dma((2, 3)),
        ],
        0,
        *weights, *moments, taps, tokens, cotangent, keeps, gains,
        vmem=62,
    )
    return found


LAG = 2


def add_rows(acc, other):
    return (acc.astype(F32) + other.astype(F32)).astype(BF16)


def backward_kernel(
    seqs, chans, held,
    ffn_g, in_full, out_full, streams, block_own,
    tokens, residual, second_grad, cotangent, keeps, gains, taps,
    result, total, input_grad, io_g, blocks, *refs
):
    bits = seqs.bit_length() - 1
    levels = bits - 1
    landed, line_land = refs[: levels + 1], refs[levels + 1]
    temps, refs = refs[levels + 2 : 2 * levels + 3], refs[2 * levels + 3 :]
    (
        acc, line_temp, sent, got, sums,
        residual_low, low_own, first_own, residual_grad, stream_own, mixed_own, mixer_grad, first_grad,
        stream, in_v, out_v, staging,
        load_sem, temp_sem, fetch_sem, c_send, c_recv, b_send, b_recv, z_send, z_recv, n_send, n_recv,
        mix_sem, io_sem, *relay_sems
    ) = refs
    parts, half_seqs = PIECES // seqs, seqs // 2
    chunks = chans * parts
    slots, group = acc.shape[0], temps[0].shape[0]
    at_once = group == half_seqs
    r, c = lax.axis_index("seq"), lax.axis_index("chan")
    core, h = lax.rem(r, 2), lax.div(r, 2)
    partners = [{"seq": flip(r, bit)} for bit in range(bits)]
    greet(partners + [{"chan": lax.rem(c + off, chans)} for off in range(1, chans)])
    partners += [{"chan": flip(c, bit)} for bit in range(chans.bit_length() - 1)]

    def slot_of(k):
        return lax.rem(k, slots)

    def core_copy(k, source):
        return remote(source.at[:, 1 - core], landed[0].at[k], c_send.at[k], c_recv.at[k], seq=flip(r, 0))

    def load(k, source):
        return pltpu.make_async_copy(source.at[:, core], acc.at[slot_of(k)], load_sem.at[k])

    def with_source(k, work):
        @pl.when(k < 3 * parts)
        def _():
            work(ffn_g.at[lax.div(k, parts), lax.rem(k, parts)])

        @pl.when(k >= 3 * parts)
        def _():
            work(io_g.at[k - 3 * parts])

    def lanes(half):
        return pl.ds(half * (D // 2), D // 2)

    def across(k, half, level):
        order = high_bits(bits, half)
        bit, rest = order[level], [one - 1 for one in order[level + 1 :]]
        base = h
        for one in rest:
            base = base - (1 << one) * lax.rem(lax.div(h, 1 << one), 2)
        first = half_seqs - (half_seqs >> level)
        copies, keeps = [], []
        for at in range(1 << len(rest)):
            place = base + sum((1 << one) for n, one in enumerate(rest) if at >> n & 1)
            copies.append(
                remote(
                    acc.at[slot_of(k), flip(place, bit - 1), :, lanes(half)],
                    landed[level + 1].at[k, at, :, lanes(half)],
                    b_send.at[k, half, first + at], b_recv.at[k, half, first + at],
                    seq=flip(r, bit),
                )
            )
            keeps.append(place)
        return copies, keeps

    def fetch(src, dst):
        copy = pltpu.make_async_copy(src, dst, temp_sem)
        copy.start()
        copy.wait()

    def begin(k):
        def work(source):
            core_copy(k, source).start()
            load(k, source).start()

        with_source(k, work)

    def level_start(k, level):
        for half in range(2):
            for copy in across(k, half, level)[0]:
                copy.start()

    def fetch_level(k, level):
        return pltpu.make_async_copy(landed[level].at[k], temps[level], fetch_sem.at[level])

    def core_arrive(k):
        load(k, io_g.at[0]).wait()
        core_copy(k, io_g.at[0]).wait_recv()
        if at_once:
            fetch_level(k, 0).start()

    def core_sum(k):
        if at_once:
            fetch_level(k, 0).wait()
        for start in range(0, half_seqs, group):
            if not at_once:
                fetch(landed[0].at[k, pl.ds(start, group)], temps[0])

            @pl.loop(0, group)
            def _(b):
                acc[slot_of(k), start + b] = add_rows(acc[slot_of(k), start + b], temps[0][b])

        level_start(k, 0)

    def level_arrive(k, level):
        for half in range(2):
            for copy in across(k, half, level)[0]:
                copy.wait_recv()
        if at_once:
            fetch_level(k, level + 1).start()

    def level_sum(k, level):
        both = [across(k, half, level) for half in range(2)]
        if at_once:
            fetch_level(k, level + 1).wait()
        temp = temps[level + 1 if at_once else 0]
        count = half_seqs >> (level + 1)
        for start in range(0, count, group):
            here = min(group, count - start)
            if not at_once:
                fetch(landed[level + 1].at[k, pl.ds(start, here)], temp.at[pl.ds(0, here)])
            for half in range(2):
                for at in range(here):
                    place = both[half][1][start + at]
                    acc[slot_of(k), place, :, lanes(half)] = add_rows(
                        acc[slot_of(k), place, :, lanes(half)], temp[at, :, lanes(half)]
                    )
        if level + 1 < levels:
            level_start(k, level + 1)

    def line(k, side):
        return remote(
            acc.at[slot_of(k), h], line_land.at[side, k], z_send.at[k], z_recv.at[side, k],
            chan=c + 1 - 2 * side,
        )

    def hop(k, step):
        keeper = lax.div(k, parts)
        for side, sends in ((0, (c < keeper) & (c == step)), (1, (c > keeper) & (chans - 1 - c == step))):

            @pl.when(sends)
            def _():
                if step > 0:
                    line(k, side).wait_recv()
                    fetch(line_land.at[side, k], line_temp.at[0])
                    acc[slot_of(k), h] = add_rows(acc[slot_of(k), h], line_temp[0])
                line(k, side).start()

    def finish(k):
        keeper = lax.div(k, parts)

        @pl.when(c == keeper)
        def _():
            for side, there in ((0, c > 0), (1, c < chans - 1)):

                @pl.when(there)
                def _():
                    line(k, side).wait_recv()
                    fetch(line_land.at[side, k], line_temp.at[side])

                @pl.when(jnp.logical_not(there))
                def _():
                    line_temp[side] = jnp.zeros(line_temp.shape[1:], BF16)

            result[lax.rem(k, parts)] = (
                acc[slot_of(k), h].astype(F32) + line_temp[0].astype(F32) + line_temp[1].astype(F32)
            ).astype(BF16)

        @pl.when(c < keeper)
        def _():
            line(k, 0).wait_send()

        @pl.when(c > keeper)
        def _():
            line(k, 1).wait_send()

        core_copy(k, io_g.at[0]).wait_send()
        for level in range(levels):
            for half in range(2):
                for copy in across(k, half, level)[0]:
                    copy.wait_send()

    def small_copy(level):
        return remote(
            sent.at[level], got.at[level], n_send.at[level], n_recv.at[level], **partners[level]
        )

    def small_step(level):
        if level == 0:
            sent[0] = sums[...]
        else:
            small_copy(level - 1).wait()
            new = sent[level - 1] + got[level - 1]
            if level == len(partners):
                total[...] = new
            else:
                sent[level] = new
        if level < len(partners):
            small_copy(level).start()

    rows, full = tokens.shape
    width = out_v.shape[-1]
    length = rows // held
    size = length - HEAD
    tile, per_tile = rows // 3, held // 3
    tiles = [pl.ds(at * tile, tile) for at in range(3)]
    own_tiles = [pl.ds(at * per_tile * size, per_tile * size) for at in range(3)]

    def mix_loads(j):
        return [
            pltpu.make_async_copy(in_full.at[j], in_v, mix_sem.at[0]),
            pltpu.make_async_copy(out_full.at[j], out_v, mix_sem.at[1]),
            pltpu.make_async_copy(streams.at[j], stream, mix_sem.at[2]),
        ]

    def io_out(j):
        at, first = lax.div(4 * j, half_seqs), lax.rem(4 * j, half_seqs)
        return pltpu.make_async_copy(staging, io_g.at[at, pl.ds(first, 4)], io_sem)

    def mix_prepare():
        gain_sum = jnp.zeros((1, full), F32)
        for at, here in enumerate(tiles):
            values = residual[here]
            scale = row_scale(values)
            unit = values * scale
            grad = second_grad[here]
            scaled = grad * gains[1:2]
            new = cotangent[here] + scale * (
                scaled - unit * jnp.mean(scaled * unit, axis=1, keepdims=True)
            )
            residual_low[here] = new.astype(BF16)
            for s, (one, two) in enumerate(
                zip(own_rows(new, per_tile), own_rows(grad * unit, per_tile))
            ):
                where = pl.ds((at * per_tile + s) * size, size)
                residual_grad[where] = one
                low_own[where] = one.astype(BF16)
                gain_sum += jnp.sum(two, axis=0, keepdims=True)
            first = tokens[here]
            first = first * row_scale(first) * gains[0:1]
            for s, one in enumerate(own_rows(first, per_tile)):
                first_own[pl.ds((at * per_tile + s) * size, size)] = one.astype(BF16)
        sums[...] = jnp.zeros_like(sums)
        sums[1:2] = gain_sum
        first_grad[...] = jnp.zeros_like(first_grad)
        staging[...] = jnp.zeros_like(staging)

    def mix_step(j):
        for copy in mix_loads(j):
            copy.wait()
        in_w, out_w = in_v[...].reshape(full, 3 * width), out_v[...].reshape(full, width)
        filters = taps[j]
        for here in tiles:
            mixer_grad[here] = dot(residual_low[here], out_w)
        input_gate, output_gate, value = (
            stream[:, k * width : (k + 1) * width] for k in range(3)
        )
        keep_one, keep_two = keeps[:, 0:1], keeps[:, 1:2]
        gated = input_gate * value
        back_one, back_two = pltpu.roll(gated, 1, 0), pltpu.roll(gated, 2, 0)
        filtered = (
            filters[2:3] * gated
            + filters[1:2] * keep_one * back_one
            + filters[0:1] * keep_two * back_two
        )
        grad = mixer_grad[...]
        inner = grad * output_gate
        one, two = keep_one * inner, keep_two * inner
        gated_grad = (
            filters[2:3] * inner
            + filters[1:2] * pltpu.roll(one, rows - 1, 0)
            + filters[0:1] * pltpu.roll(two, rows - 2, 0)
        )

        def own_sum(values):
            return sum(jnp.sum(part, axis=0, keepdims=True) for part in own_rows(values, held))

        where = pl.ds(pl.multiple_of(j * width, width), width)
        sums[4:5, where] = own_sum(inner * gated)
        sums[3:4, where] = own_sum(one * back_one)
        sums[2:3, where] = own_sum(two * back_two)
        for k, values in enumerate((gated_grad * value, grad * filtered, gated_grad * input_gate)):
            for s, part in enumerate(own_rows(values, held)):
                stream_own[pl.ds(s * size, size), k * width : (k + 1) * width] = part.astype(BF16)
        for s, part in enumerate(own_rows(output_gate * filtered, held)):
            mixed_own[pl.ds(s * size, size)] = part.astype(BF16)
        for here in own_tiles:
            first_grad[here] += contract_last(stream_own[here], in_w)

        @pl.when(j > 0)
        def _():
            io_out(j - 1).wait()

        for k in range(4):
            if k < 3:
                new = contract_first(stream_own[:, k * width : (k + 1) * width], first_own[...])
            else:
                new = contract_first(mixed_own[...], low_own[...])
            staging[k, :, pl.ds(0, SMALL_PIECE)] = new.astype(BF16).reshape(2, SMALL_PIECE, full)
        io_out(j).start()

        @pl.when(j + 1 < chans)
        def _():
            for copy in mix_loads(j + 1):
                copy.start()

    def mix_end():
        gain_sum = jnp.zeros((1, full), F32)
        for s in range(held):
            here = pl.ds(s * size, size)
            values = tokens[pl.ds(s * length + HEAD, size)]
            scale = row_scale(values)
            unit = values * scale
            grad = first_grad[here]
            scaled = grad * gains[0:1]
            gain_sum += jnp.sum(grad * unit, axis=0, keepdims=True)
            input_grad[here] = (
                residual_grad[here]
                + scale * (scaled - unit * jnp.mean(scaled * unit, axis=1, keepdims=True))
            ).astype(BF16)
        sums[0:1] = gain_sum
        io_out(chans - 1).wait()

    spread_out = parts == 4
    mix_first, mix_last = (1, 3 * parts - 2) if spread_out else (-1, -1)
    relay = Relay(chans, block_own, blocks, relay_sems)
    for copy in mix_loads(0):
        copy.start()
    begin(0)
    relay.step(0)
    mix_prepare()
    if not spread_out:

        @pl.loop(0, chans)
        def _(j):
            mix_step(j)

        mix_end()

    summed = LAG * (1 + levels)

    @pl.loop(1, chunks + summed + LAG * (chans - 1))
    def _(tick):
        def stage(k, work):
            @pl.when((k >= 0) & (k < chunks))
            def _():
                work(k)

        stage(tick - summed - LAG * (chans - 1), finish)
        stage(tick, begin)
        for step in range(chans - 2, 0, -1):
            stage(tick - summed - LAG * step, lambda k: hop(k, step))
        for level in range(levels - 1, -1, -1):
            stage(tick - LAG * (2 + level), lambda k: level_arrive(k, level))
        stage(tick - LAG, core_arrive)
        for level in range(levels - 1, -1, -1):

            def work(k):
                level_sum(k, level)
                if level == levels - 1:
                    hop(k, 0)

            stage(tick - LAG * (2 + level), work)
        stage(tick - LAG, core_sum)
        if spread_out:

            @pl.when((tick >= mix_first) & (tick < mix_first + 2 * chans) & (lax.rem(tick - mix_first, 2) == 0))
            def _():
                mix_step(lax.div(tick - mix_first, 2))

            @pl.when(tick == mix_last)
            def _():
                mix_end()

        for level in range(len(partners) + 1):

            @pl.when(tick == mix_last + 2 + level)
            def _():
                small_step(level)

        for step in (1, 2):

            @pl.when(tick == 7 * step)
            def _():
                relay.step(step)

    relay.finish()


def backward_pass(
    seqs, chans, held, ffn_g, in_full, out_full, streams, block_own, tokens, residual, second_grad,
    cotangent, keeps, gains, taps,
):
    dma, vmem, shape = pltpu.SemaphoreType.DMA, pltpu.VMEM, jax.ShapeDtypeStruct
    parts, half_seqs = PIECES // seqs, seqs // 2
    levels = seqs.bit_length() - 2
    chunks = chans * parts
    slots = min(chunks, LAG * (levels + chans) + 1)
    group = min(4, half_seqs)
    sizes = [group] + [half_seqs >> level if group == half_seqs else 1 for level in range(1, levels + 1)]
    partners = (seqs * chans).bit_length() - 1
    rows, width = tokens.shape
    own_count = rows - held * HEAD
    part = out_full.shape[-1]
    outs = [
        shape((parts, PIECE, D), BF16),
        shape((8, width), F32),
        shape((own_count, width), BF16),
        shape((parts, half_seqs, 2, PIECE, D), BF16),
        shape((chans,) + block_own.shape, BF16),
        shape((chunks, half_seqs, PIECE, D), BF16),
    ]
    outs += [
        shape((chunks, half_seqs >> (level + 1), PIECE, D), BF16) for level in range(levels)
    ]
    outs.append(shape((2, chunks, PIECE, D), BF16))
    return call(
        functools.partial(backward_kernel, seqs, chans, held),
        outs,
        [pl.ANY] * 5 + [vmem] * 7,
        [vmem] * 3 + [pl.ANY] * (len(outs) - 3),
        [
            *[vmem((size, PIECE, D), BF16) for size in sizes],
            vmem((slots, half_seqs, PIECE, D), BF16),
            vmem((2, PIECE, D), BF16),
            vmem((partners, 8, width), F32),
            vmem((partners, 8, width), F32),
            vmem((8, width), F32),
            vmem((rows, width), BF16),
            vmem((own_count, width), BF16),
            vmem((own_count, width), BF16),
            vmem((own_count, width), F32),
            vmem((own_count, 3 * part), BF16),
            vmem((own_count, part), BF16),
            vmem((rows, part), F32),
            vmem((own_count, width), F32),
            vmem((rows, 3 * part), F32),
            vmem(in_full.shape[1:], BF16),
            vmem(out_full.shape[1:], BF16),
            vmem((4, 2, PIECE, D), BF16),
            dma((chunks,)),
            dma(()),
            dma((levels + 1,)),
            dma((chunks,)),
            dma((chunks,)),
            dma((chunks, 2, half_seqs)),
            dma((chunks, 2, half_seqs)),
            dma((chunks,)),
            dma((2, chunks)),
            dma((partners,)),
            dma((partners,)),
            dma((3,)),
            dma(()),
            *Relay.semaphores(chans),
        ],
        1,
        ffn_g.reshape(3, parts, half_seqs, 2, PIECE, D),
        in_full, out_full, streams, block_own, tokens, residual, second_grad, cotangent, keeps, gains,
        taps,
        vmem=62,
    )[:5]


def shifted(value, axes, by):
    length = lax.axis_size(axes)
    pairs = [(i, i + by) for i in range(length) if 0 <= i + by < length]
    return lax.ppermute(value, axes, pairs)


def adam_update(param, gradient, first, second):
    first_new = FIRST_DECAY * first + (1.0 - FIRST_DECAY) * gradient
    second_new = SECOND_DECAY * second + (1.0 - SECOND_DECAY) * gradient * gradient
    first_fix = 1.0 - FIRST_DECAY**STEP
    second_fix = 1.0 - SECOND_DECAY**STEP
    param_new = param - ADAM_RATE * (first_new / first_fix) / (
        jnp.sqrt(second_new / second_fix) + ADAM_EPS
    )
    return (param_new, first_new, second_new)


COLUMNS = [3 * D, D, FF, FF, FF]
RATES = [1.0, 1.0, 1.0, 1.0, 0.5]


def last_kernel(block_low, input_low, grad_home, ortho_home, *refs):
    weights, moments, (block_out, input_grad) = refs[:5], refs[5:10], refs[10:12]
    moments_new, weights_new = refs[12:22:2], refs[13:22:2]
    step = pl.program_id(0)
    for low, whole in ((block_low, block_out), (input_low, input_grad)):
        rows = low.shape[2]
        for at in range(low.shape[0]):
            whole[0, at * rows : (at + 1) * rows] = low[at, 0].astype(F32)

    def update(index, at, lanes, grad, ortho):
        rate = RATES[index]
        here = at + (slice(None), lanes)
        moments_new[index][here] = MOMENTUM_DECAY * moments[index][here] + grad.astype(F32).T
        weights_new[index][here] = (
            weights[index][here] * (1.0 - WEIGHT_DECAY * rate)
            - rate * math.sqrt(COLUMNS[index] / D) * ortho.astype(F32).T
        )

    for m in range(3):

        @pl.when(step == m)
        def _():
            for t in range(TILES):
                rows = slice(t * UNIT, (t + 1) * UNIT)
                update(
                    m + 2, (), slice(t * LANES, (t + 1) * LANES),
                    *(home[m, :, rows].reshape(LANES, -1) for home in (grad_home, ortho_home)),
                )

    @pl.when(step == 3)
    def _():
        for q in range(PER_CHAN):
            lanes = slice(q % 2 * SMALL_PIECE, (q % 2 + 1) * SMALL_PIECE)
            blocks = [home[3, q, 0:SMALL_PIECE] for home in (grad_home, ortho_home)]
            update(*((0, (q // 2,)) if q < IN_PIECES else (1, ())), lanes, *blocks)


def last_pass(block_low, input_low, homes, weights, moments):
    chans, held, sub, width = block_low.shape
    low = pl.BlockSpec((chans, 1, sub, width), lambda s: (0, s, 0, 0))
    whole = pl.BlockSpec((1, chans * sub, width), lambda s: (s, 0, 0))

    def all_of(array):
        return pl.BlockSpec(array.shape, lambda s: (0,) * array.ndim)

    shape = jax.ShapeDtypeStruct
    outs = [shape((held, chans * sub, width), F32)] * 2
    out_specs = [whole] * 2
    for weight in weights:
        outs += [shape(weight.shape, F32)] * 2
        out_specs += [all_of(weight)] * 2
    return pl.pallas_call(
        last_kernel,
        grid=(held,),
        out_shape=outs,
        in_specs=[low] * 2 + [all_of(one) for one in (*homes, *weights, *moments)],
        out_specs=out_specs,
        compiler_params=pltpu.CompilerParams(vmem_limit_bytes=60 * 1024 * 1024),
    )(block_low, input_low, *homes, *weights, *moments)


def on_device(
    tokens,
    segment_ids,
    cotangent,
    norm_gains,
    filter_weight,
    in_weight,
    out_weight,
    gate_weight,
    up_weight,
    down_weight,
    norm_gains_mean,
    norm_gains_square,
    filter_mean,
    filter_square,
    in_momentum,
    out_momentum,
    gate_momentum,
    up_momentum,
    down_momentum,
):
    seqs, chans = lax.axis_size("seq"), lax.axis_size("chan")
    r, c = lax.axis_index("seq"), lax.axis_index("chan")
    seq_total, local_rows, width = tokens.shape
    sub = local_rows // chans
    chan_width = filter_weight.shape[1]

    weights = [in_weight.transpose(1, 0, 2), out_weight, gate_weight, up_weight, down_weight]
    moments = [
        in_momentum.transpose(1, 0, 2), out_momentum, gate_momentum, up_momentum, down_momentum
    ]

    def share(array, start, length):
        return lax.dynamic_slice_in_dim(array, start, length, axis=1)

    positions = r * local_rows + jnp.arange(local_rows, dtype=jnp.int32)
    local_keeps = jnp.stack(
        [(segment_ids <= positions[None, :] - offset).astype(F32) for offset in (1, 2)], axis=-1
    )
    following = jnp.where(
        c == chans - 1,
        shifted(local_keeps[:, :2], "seq", -1),
        share(local_keeps, lax.rem(c + 1, chans) * sub, 2),
    )
    following = jnp.concatenate([following[-1:], following[:-1]])
    gap = jnp.zeros((seq_total, HEAD - 2, 2), F32)
    keeps = jnp.concatenate([following, gap, share(local_keeps, c * sub, sub)], axis=1).reshape(-1, 2)

    (
        in_full, out_full, _, taps, moments_held, _, streams, ffn_grads,
        token_rows, upstream_rows, residual, second_grad, block_out,
    ) = forward_pass(
        seqs, chans, weights, moments, filter_weight, tokens, cotangent, keeps, norm_gains
    )
    moments_held = moments_held.transpose(0, 2, 1, 3).reshape(-1, D)
    grads_held, small, input_grad, _, block_out = backward_pass(
        seqs, chans, seq_total, ffn_grads, in_full, out_full, streams, block_out, token_rows, residual,
        second_grad, upstream_rows, keeps, norm_gains, taps,
    )

    gains_new, gains_mean_new, gains_square_new = adam_update(
        norm_gains, small[:2], norm_gains_mean, norm_gains_square
    )
    filter_new, filter_mean_new, filter_square_new = adam_update(
        filter_weight, share(small[2:5], c * chan_width, chan_width), filter_mean, filter_square
    )

    *homes, input_grad = orthogonalize(
        seqs, chans, grads_held.reshape(-1, D), moments_held, input_grad
    )
    block_out, input_grad = (
        one.reshape(chans, seq_total, sub, width) for one in (block_out, input_grad)
    )
    block_out, input_grad, *results = last_pass(block_out, input_grad, homes, weights, moments)
    results[:2] = [one.transpose(1, 0, 2) for one in results[:2]]
    return (
        block_out,
        input_grad,
        gains_new,
        gains_mean_new,
        gains_square_new,
        filter_new,
        filter_mean_new,
        filter_square_new,
        *results,
    )


def solution(mesh):
    return jax.shard_map(
        on_device,
        mesh=mesh,
        in_specs=(
            P(None, "seq", None),
            P(None, "seq"),
            P(None, "seq", None),
            P(),
            P(None, "chan"),
            P("seq", None, "chan"),
            P("seq", "chan"),
            P("seq", "chan"),
            P("seq", "chan"),
            P("seq", "chan"),
            P(),
            P(),
            P(None, "chan"),
            P(None, "chan"),
            P("seq", None, "chan"),
            P("seq", "chan"),
            P("seq", "chan"),
            P("seq", "chan"),
            P("seq", "chan"),
        ),
        out_specs=(
            P(None, "seq", None),
            P(None, "seq", None),
            P(),
            P(),
            P(),
            P(None, "chan"),
            P(None, "chan"),
            P(None, "chan"),
            P("seq", None, "chan"),
            P("seq", None, "chan"),
            P("seq", "chan"),
            P("seq", "chan"),
            P("seq", "chan"),
            P("seq", "chan"),
            P("seq", "chan"),
            P("seq", "chan"),
            P("seq", "chan"),
            P("seq", "chan"),
        ),
        check_vma=False,
    )
```

time: 2700 us -> 674 us (0.25)
  waiting for transfers between devices: 2080 us -> 1.64 us
  Pallas kernels: 0 us -> 658 us
  matrix products: 292 us -> 0 us
  other arithmetic: 135 us -> 2.91 us
  blocking collectives: 115 us -> 0 us
  local copies, waits for them, and re-layouts: 45.2 us -> 4.72 us
    psum x6 -> x0, waiting for transfers between devices: 1050 us -> none  [the longest x1 474 us: on_device(): lax.psum(contract_last(activated, down_full).astype(jnp.bfloat16), 'chan')]
    all_gather x40 -> x0, waiting for transfers between devices: 882 us -> none  [the longest x4 114 us: on_device(): lax.all_gather(states[4], 'seq', axis=0, tiled=True)]
    pallas_call x0 -> x4, Pallas kernels: none -> 658 us  [the longest x3 641 us: call(): pl.pallas_call(kernel, out_shape=outs, in_specs=[pl.BlockSpec(memory_spac...]
    dot_general x55 -> x0, matrix products: 292 us -> none  [the longest x25 110 us: contract_last(): lax.dot_general(left, right, (((1,), (1,)), ((), ())), preferred_element_...]
    reduce_scatter x5 -> x0, waiting for transfers between devices: 136 us -> none  [the longest x1 44.2 us: on_device(): lax.psum_scatter(down_weight_grad.astype(jnp.bfloat16), 'seq', scatter_di...]
    psum x2 -> x0, blocking collectives: 63.4 us -> none  [the longest x1 39.7 us: on_device(): totals = lax.psum(squares, ('seq', 'chan'))]
    all_gather x5 -> x0, blocking collectives: 51.4 us -> none  [the longest x4 41.2 us: on_device(): lax.all_gather(states[1], 'seq', axis=0, tiled=True)]
    add x4 -> x0, other arithmetic: 46.8 us -> none  [the longest x1 16.4 us: on_device(): residual_grad + first_scale * (first_scaled - first_unit * jnp.mean(first...]
  transfers between devices with their start and end apart: 53 -> 1, of which waited for: 48 -> 1; matrix products, arithmetic and copies ran while one was open for 13% -> 0% of each run, Pallas kernels for 0% -> 0%
where the time goes in v1:
time: 674 us; the launch traced here: 670 us
  Pallas kernels  658 us (98%)
    pallas_call x3, Pallas kernels, call(): pl.pallas_call(kernel, out_shape=outs, in_specs=[pl.BlockSpec(memory_spac...  641 us
    pallas_call x1, Pallas kernels, last_pass(): pl.pallas_call(last_kernel, grid=(held,), out_shape=outs, in_specs=[low]...  17.6 us
  transfers between devices with their start and end apart: 1, of which 1 were waited for; matrix products, arithmetic and copies ran while one was open for 0% of the time, Pallas kernels for 0%

profile of v1, /device:TPU:0, one launch (start us, length us, event | category | flops | bytes accessed | tf_op | source)
XLA Modules:
  0.0 669.9 jit_solution(12099261700401816626)
XLA Ops:
  0.7 0.7 compare_bitcast_fusion.1
  1.4 1.3 collective-permute-start
  2.8 0.1 pad.2.clone
  2.8 1.6 collective-permute-done
  4.5 0.1 dynamic-slice_select_fusion
  4.6 0.1 pad_maximum_fusion
  4.6 1.0 copy.48
  5.6 234.2 %shard_map.322 = (bf16[4,8,128,768]{3,2,1,0:T(8,128)(2,1)}, bf16[4,8,128,256]{3,2,1,0:T(8,128)(2,1)}, bf16[9,4,8,3,128,128]{5,4,3,2,1,0:T(8,128)(2,1)}, f32[4,8,...) custom-call(f32[3,128,256]{2,1,0:T(8,128)} %bitcast.28, ...), custom_call_target="tpu_custom_call" | custom-call | tf_op jit(solution)/shard_map/pallas_call | solution.py:74
  239.8 0.0 copy-start.3
  239.8 217.5 %shard_map.323 = (bf16[4,144,1024]{2,1,0:T(8,128)(2,1)}, f32[8,1024]{1,0:T(8,128)}, bf16[768,1024]{1,0:T(8,128)(2,1)}, bf16[4,4,2,144,1024]{4,3,2,1,0:T(8,128)(2...) custom-call(bf16[3,4,4,2,144,1024]{5,4,3,2,1,0:T(8,128)(2,1)} %bitca, ...), custom_call_target="tpu_custom_call" | custom-call | tf_op jit(solution)/shard_map/pallas_call | solution.py:74
  457.3 0.0 copy-start.4
  457.3 0.0 copy-start.6
  457.3 0.0 copy-start.7
  457.3 0.0 copy-start.2
  457.4 0.0 copy-start.5
  457.4 0.0 copy-start.8
  457.4 0.0 copy-start.9
  457.4 0.9 slice.19
  458.2 0.0 copy-done.3
  458.3 0.3 copy.49
  458.6 0.3 copy.52
  458.9 0.0 copy-done.4
  458.9 0.0 copy-done.6
  458.9 0.0 copy-done.7
  458.9 1.4 divide_subtract_fusion
  460.3 0.0 copy-done.2
  460.3 189.0 %shard_map.324 = (bf16[4,8,144,128]{3,2,1,0:T(8,128)(2,1)S(1)}, bf16[4,8,144,128]{3,2,1,0:T(8,128)(2,1)S(1)}, bf16[4,768,1024]{2,1,0:T(8,128)(2,1)}) custom-call(bf16[576,1024]{1,0:T(8,128)(2,1)S(1)} %bitcast.21, bf16[576,1024]{1,0:T(8,128)(2,1)S(1)} %bitcast.20, bf16[768,1024]{1,0:T(8,128)(2,1)} %get-tuple-element.61.input_grad), custom_call_target="tpu_custom_call" | custom-call | tf_op jit(solution)/shard_map/pallas_call | solution.py:74
  649.3 0.0 copy-start
  649.3 1.0 copy-done
  650.3 0.0 copy-start.1
  650.3 1.1 copy-done.1
  651.4 0.0 copy-done.5
  651.4 0.0 copy-done.8
  651.4 0.0 copy-done.9
  651.4 0.6 divide_subtract_fusion.1
  652.1 17.6 %shard_map.325 = (f32[6,512,1024]{2,1,0:T(8,128)}, f32[6,512,1024]{2,1,0:T(8,128)}, f32[3,128,256]{2,1,0:T(8,128)}, f32[3,128,256]{2,1,0:T(8,128)}, f32[128,256]...) custom-call(bf16[4,6,128,1024]{3,2,1,0:T(8,128)(2,1)} %bitcast.23, ...), custom_call_target="tpu_custom_call" | custom-call | tf_op jit(solution)/shard_map/pallas_call | solution.py:1635
  (6 shorter events, 0.0 us)
Async XLA Ops:
  1.4 3.1 collective-permute-start
  239.8 218.4 %copy-start.3 = (bf16[4,8,144,128]{3,2,1,0:T(8,128)(2,1)S(1)}, bf16[4,8,144,128]{3,2,1,0:T(8,128)(2,1)}, u32[]{:S(2)}) copy-start(bf16[4,8,144,128]{3,2,1,0:T(8,128)(2,1)} %get-tuple-element.60) | copy-start | bytes 3538948
  457.3 1.6 copy-start.4
  457.3 1.6 copy-start.6
  457.3 1.6 copy-start.7
  457.3 3.0 copy-start.2
  457.4 194.1 %copy-start.5 = (f32[3,256]{1,0:T(4,128)S(1)}, f32[3,256]{1,0:T(4,128)}, u32[]{:S(2)}) copy-start(f32[3,256]{1,0:T(4,128)} %refs_10_.1) | copy-start | bytes 9220
  457.4 194.1 %copy-start.8 = (f32[3,256]{1,0:T(4,128)S(1)}, f32[3,256]{1,0:T(4,128)}, u32[]{:S(2)}) copy-start(f32[3,256]{1,0:T(4,128)} %param.31) | copy-start | bytes 9220
  457.4 194.1 %copy-start.9 = (f32[3,256]{1,0:T(4,128)S(1)}, f32[3,256]{1,0:T(4,128)}, u32[]{:S(2)}) copy-start(f32[3,256]{1,0:T(4,128)} %param.32) | copy-start | bytes 9220
  649.3 1.0 copy-start
  650.3 1.1 copy-start.1

commit v2 on v1

--- a/solution.py
+++ b/solution.py
@@ -70,13 +70,14 @@
     return order if half == 0 else order[::-1]
 
 
-def call(kernel, outs, in_spaces, out_spaces, scratch, ident, *args, vmem=48):
+def call(kernel, outs, in_spaces, out_spaces, scratch, ident, *args, vmem=48, aliases=None):
     return pl.pallas_call(
         kernel,
         out_shape=outs,
         in_specs=[pl.BlockSpec(memory_space=space) for space in in_spaces],
         out_specs=jax.tree.map(lambda space: pl.BlockSpec(memory_space=space), out_spaces),
         scratch_shapes=scratch,
+        input_output_aliases=aliases or {},
         compiler_params=pltpu.CompilerParams(
             collective_id=ident, has_side_effects=True, vmem_limit_bytes=vmem * 1024 * 1024
         ),
@@ -208,14 +209,14 @@
             @pl.when(comes)
             def _():
                 remote(
-                    self.own, self.blocks.at[block], self.send.at[side, hop], self.recv.at[side, hop],
-                    chan=c - 1 + 2 * side,
+                    self.blocks.at[block], self.blocks.at[block],
+                    self.send.at[side, hop], self.recv.at[side, hop], chan=c - 1 + 2 * side,
                 ).wait_recv()
 
-    def step(self, hop):
+    def step(self, hop, first=False):
         if hop == 0:
             self.keeping().start()
-        else:
+        elif not first:
             self.await_hop(hop - 1)
         for sends, copy in self.copies(hop):
 
@@ -223,10 +224,11 @@
             def _():
                 copy.start()
 
-    def finish(self):
-        self.await_hop(self.chans - 2)
-        self.keeping().wait()
-        for hop in range(self.chans - 1):
+    def finish(self, hops):
+        self.await_hop(hops[-1])
+        if 0 in hops:
+            self.keeping().wait()
+        for hop in hops:
             for sends, copy in self.copies(hop):
 
                 @pl.when(sends)
@@ -252,7 +254,7 @@
 
 
 def ortho_kernel(
-    seqs, chans, grad, moment, input_grad, grad_home, ortho_home, input_blocks,
+    seqs, chans, grad, moment, _, grad_home, ortho_home, input_blocks,
     out, cut_grad, cut_ortho, between_grad, between_ortho,
     part, own, swapped, paired, parts, sums, gram, poly, half_way,
     x_send, x_recv, s_send, s_recv, g_send, g_recv, f_send, f_recv, *home_sems
@@ -269,7 +271,7 @@
     )
     home_grad = Homeward(seqs, chans, cut_grad, grad_home, between_grad, home_sems[:6])
     home_ortho = Homeward(seqs, chans, cut_ortho, ortho_home, between_ortho, home_sems[6:12])
-    relay = Relay(chans, input_grad, input_blocks, home_sems[12:])
+    relay = Relay(chans, None, input_blocks, home_sems[12:])
     columns = out.shape[0]
     slab = PIECE
 
@@ -282,7 +284,7 @@
 
     for at in range(columns // slab):
         home_grad.drop(at)
-    relay.step(0)
+    relay.step(1, first=True)
 
     apart = c == chans - 1
 
@@ -381,8 +383,6 @@
             share(peer).wait_send()
         for pair in [h] + peers:
             forward(pair).wait_send()
-        if turn == 1:
-            relay.step(2)
 
         scale = jnp.ones((1, 1), F32)
         if turn == 0:
@@ -444,21 +444,21 @@
 
         if turn == 0:
             home_grad.spread()
-            relay.step(1)
+            relay.step(2)
 
     home_ortho.spread()
     home_grad.finish()
-    relay.finish()
+    relay.finish(range(1, chans - 1))
     home_ortho.finish()
 
 
-def orthogonalize(seqs, chans, grad, moment, input_grad):
+def orthogonalize(seqs, chans, grad, moment, input_blocks):
     dma = pltpu.SemaphoreType.DMA
     count, block, held = seqs // 2, D // seqs, PIECES // seqs
     return call(
         functools.partial(ortho_kernel, seqs, chans),
         [jax.ShapeDtypeStruct((chans, PER_CHAN, PIECE, block), BF16)] * 2
-        + [jax.ShapeDtypeStruct((chans,) + input_grad.shape, BF16)],
+        + [jax.ShapeDtypeStruct(input_blocks.shape, BF16)],
         [pltpu.VMEM] * 2 + [pl.ANY],
         [pl.ANY] * 3,
         [
@@ -485,7 +485,8 @@
         2,
         grad,
         moment,
-        input_grad,
+        input_blocks,
+        aliases={2: 2},
     )
 
 
@@ -513,31 +514,29 @@
 def forward_work(
     seqs, chans, held,
     weights, moments, own_taps, token_source, cotangent_source, keeps, gains,
-    in_full, out_full, ffn_full, taps_all, held_out, between, streams, ffn_g,
+    io_full, ffn_full, taps_all, held_out, between, streams, ffn_g,
     tokens, cotangent, residual, second_grad, block_out,
-    in_shard, out_shard, ffn_shard, taps, packed, shelf, shelf_sem,
-    u, u_own, halo, row_sem, halo_sem, halo_send, halo_recv, normed, mixed, stream, x, x_own, ffn_out, act, gate_low, up_low, in_v, out_v, taps_v, w_v, grad_v,
+    io_shard, ffn_shard, taps, packed, shelf, shelf_sem,
+    io_own, p_send, p_recv, q_send, q_recv, line_send, line_recv,
+    u, u_own, halo, row_sem, halo_sem, halo_send, halo_recv, normed, mixed, stream, x, x_own, ffn_out, act, gate_low, up_low, io_v, taps_v, w_v, grad_v,
     own_sem, z_send, z_recv, b_send, b_recv, c_send, c_recv,
     t_own, t_send, t_recv, p_own, ps_send, ps_recv, pl_send, pl_recv,
     mix_sem, taps_sem, stream_sem, load_sem, grad_sem,
 ):
     bits = seqs.bit_length() - 1
     r, c = lax.axis_index("seq"), lax.axis_index("chan")
-    last = TILES + 1
+    last = TILES - 1
+    pair, mine = lax.div(r, 2), lax.rem(r, 2)
     greet(
         [{"chan": lax.rem(c + off, chans)} for off in range(1, chans)]
         + [{"seq": lax.rem(r + off, seqs)} for off in range(1, seqs)]
     )
 
     def shard(k):
-        if isinstance(k, int) and k < 2:
-            return (in_shard, out_shard)[k]
-        return ffn_shard.at[k - 2]
+        return ffn_shard.at[k]
 
     def full(k, part, block):
-        if isinstance(k, int) and k < 2:
-            return (in_full, out_full)[k].at[part, block]
-        return ffn_full.at[k - 2, part, block]
+        return ffn_full.at[k, part, block]
 
     def own(k):
         return pltpu.make_async_copy(shard(k), full(k, c, r), own_sem.at[k])
@@ -690,18 +689,109 @@
                     lift(m).wait_send()
 
     rows, width = tokens.shape
-    part = out_full.shape[-1]
+    part = io_full.shape[-1] // 4
     tile = rows // 3
     per_tile = held // 3
     size = rows // held - HEAD
     tiles = [pl.ds(at * tile, tile) for at in range(3)]
 
-    def mix_loads(j):
-        slot = lax.rem(j, 2)
+    io_block = io_shard.shape[0] // 2
+
+    def io_keep():
+        return pltpu.make_async_copy(io_shard, io_full.at[c, pair, mine], io_own)
+
+    def io_across(half, level, incoming):
+        order = high_bits(bits, half)
+        bit, done = order[level], [one - 1 for one in order[:level]]
+        base = flip(pair, bit - 1) if incoming else pair
+        where = pl.ds(half * io_block, io_block)
+        first = (1 << level) - 1
         return [
-            pltpu.make_async_copy(in_full.at[j], in_v.at[slot], mix_sem.at[slot, 0]),
-            pltpu.make_async_copy(out_full.at[j], out_v.at[slot], mix_sem.at[slot, 1]),
+            remote(
+                io_shard.at[where] if level == 0 and not incoming else io_full.at[c, block, mine, where],
+                io_full.at[c, block, mine, where],
+                p_send.at[half, first + at], p_recv.at[half, first + at], seq=flip(r, bit),
+            )
+            for at, block in enumerate(flips(base, done))
         ]
+
+    def io_level(level):
+        for half in range(2):
+            if level > 0:
+                for copy in io_across(half, level - 1, True):
+                    copy.wait_recv()
+            if level < bits - 1:
+                for copy in io_across(half, level, False):
+                    copy.start()
+
+    def io_core(quarter, core):
+        return remote(
+            io_full.at[quarter, :, core], io_full.at[quarter, :, core],
+            q_send.at[quarter], q_recv.at[quarter], seq=flip(r, 0),
+        )
+
+    def io_sides(hop, arriving):
+        away = hop + 1 if arriving else hop
+        return (
+            (0, c - away, (c >= away) & ((c < chans - 1) | arriving)),
+            (1, c + away, (c + away < chans) & ((c > 0) | arriving)),
+        )
+
+    def io_line(side, quarter, hop):
+        return remote(
+            io_full.at[quarter, :, mine], io_full.at[quarter, :, mine],
+            line_send.at[side, hop], line_recv.at[side, hop], chan=c + 1 - 2 * side,
+        )
+
+    def io_line_in(side, quarter, hop):
+        return remote(
+            io_full.at[quarter, :, mine], io_full.at[quarter, :, mine],
+            line_send.at[side, hop], line_recv.at[side, hop], chan=c - 1 + 2 * side,
+        )
+
+    def io_start(hop):
+        for side, quarter, does in io_sides(hop, False):
+
+            @pl.when(does)
+            def _():
+                io_line(side, quarter, hop).start()
+
+    def io_arrive(hop):
+        for side, quarter, does in io_sides(hop, True):
+
+            @pl.when(does)
+            def _():
+                io_line_in(side, quarter, hop).wait_recv()
+                io_core(quarter, mine).start()
+
+        if hop + 1 < chans - 1:
+            io_start(hop + 1)
+
+    def io_sent():
+        for half in range(2):
+            for level in range(bits - 1):
+                for copy in io_across(half, level, False):
+                    copy.wait_send()
+        for hop in range(chans - 1):
+            for side, quarter, does in io_sides(hop, False):
+
+                @pl.when(does)
+                def _():
+                    io_line(side, quarter, hop).wait_send()
+
+        for quarter in range(chans):
+            io_core(quarter, mine).wait_send()
+
+    def reached(hops):
+        return jnp.minimum(c, hops) + jnp.minimum(chans - 1 - c, hops) + 1
+
+    def quarter_at(n):
+        quarter = jnp.int32(0)
+        for place in range(chans):
+            order = sorted(range(chans), key=lambda one: (abs(one - place), one))
+            for at, one in enumerate(order):
+                quarter = quarter + jnp.where((c == place) & (n == at), one, 0)
+        return quarter
 
     def stream_out(j):
         return pltpu.make_async_copy(stream, streams.at[j], stream_sem)
@@ -791,30 +881,23 @@
             normed[here] = (values * row_scale(values) * gains[0:1]).astype(BF16)
             residual[here] = values
 
-    def mix():
-        for copy in mix_loads(0):
-            copy.start()
-        copy = pltpu.make_async_copy(taps_all, taps_v, taps_sem)
-        copy.start()
-        copy.wait()
-
-        @pl.loop(0, chans)
-        def _(j):
-            slot = lax.rem(j, 2)
-            for copy in mix_loads(j):
-                copy.wait()
-
-            @pl.when(j + 1 < chans)
-            def _():
-                for copy in mix_loads(j + 1):
-                    copy.start()
-
-            @pl.when(j > 0)
-            def _():
-                stream_out(j - 1).wait()
-
-            in_w = in_v[slot].reshape(width, 3 * part)
-            out_w = out_v[slot].reshape(width, part)
+    def mix_some(hops):
+        first = 0 if hops == 0 else reached(hops - 1)
+
+        @pl.loop(first, reached(hops))
+        def _(n):
+            j = quarter_at(n)
+            io_core(j, 1 - mine).wait_recv()
+            load = pltpu.make_async_copy(io_full.at[j], io_v, mix_sem)
+            load.start()
+
+            @pl.when(n > 0)
+            def _():
+                stream_out(j).wait()
+
+            load.wait()
+            in_w = io_v[:, :, :, 0 : 3 * part].reshape(width, 3 * part)
+            out_w = io_v[:, :, :, 3 * part :].reshape(width, part)
             for here in tiles:
                 stream[here] = dot(normed[here], in_w)
             filters = taps_v[j]
@@ -825,6 +908,7 @@
             for here in tiles:
                 residual[here] += contract_last(mixed[here], out_w)
 
+    def mix_finish():
         for at, here in enumerate(tiles):
             values = residual[here]
             new = values * row_scale(values) * gains[1:2]
@@ -833,7 +917,7 @@
                 x_own[pl.ds((at * per_tile + s) * size, size)] = one.astype(BF16)
             ffn_out[here] = jnp.zeros((tile, width), F32)
             second_grad[here] = jnp.zeros((tile, width), F32)
-        stream_out(chans - 1).wait()
+        stream_out(c).wait()
 
     def loads(t):
         slot = lax.rem(t, 2)
@@ -854,8 +938,14 @@
             for m in range(3)
         ]
 
-    def feed_forward(t):
+    def feed_forward(t, arrived_last):
         slot = lax.rem(t, 2)
+
+        @pl.when(t + 1 <= arrived_last)
+        def _():
+            for copy in loads(t + 1):
+                copy.start()
+
         for copy in loads(t):
             copy.wait()
 
@@ -903,12 +993,7 @@
     def shelves(n):
         return shelf_copies(weights if n < 4 else moments, n)
 
-    for copy in shelves(0):
-        copy.start()
-    taps[...] = jnp.zeros_like(taps)
-    taps[0:3] = own_taps[...]
-    rows_start()
-    for n in range(8):
+    def shelve(n):
         if n < 7:
             for copy in shelves(n + 1):
                 copy.start()
@@ -916,10 +1001,7 @@
             copy.wait()
         slot, m = n % 2, n % 4 - 1
         if n == 0:
-            in_shard[...] = shelf[slot, :, : 3 * part].astype(BF16)
-            out_shard[...] = shelf[slot, :, 3 * part : 4 * part].astype(BF16)
-            start_chan(0)
-            start_chan(1)
+            io_shard[...] = shelf[slot, :, : 4 * part].astype(BF16)
         elif n < 4:
             for t in range(TILES):
                 ffn_shard[t, m] = shelf[slot, :, t * LANES : (t + 1) * LANES].astype(BF16)
@@ -932,14 +1014,42 @@
             for t in range(TILES):
                 block = shelf[slot, :, t * LANES : (t + 1) * LANES].T.astype(BF16)
                 packed[m, :, t * UNIT : (t + 1) * UNIT] = block.reshape(PER_CHAN, UNIT, -1)
-    pieces_start()
+
+    for copy in shelves(0):
+        copy.start()
+    taps[...] = jnp.zeros_like(taps)
+    taps[0:3] = own_taps[...]
+    shelve(0)
+    io_keep().start()
+    io_level(0)
+    rows_start()
     taps_own = pltpu.make_async_copy(taps, taps_all.at[c], t_own)
     taps_own.start()
     for off in range(1, chans):
         taps_copy(off, False).start()
+    for n in (1, 2, 3):
+        shelve(n)
+    start_chan(0)
+    io_keep().wait()
+    for level in range(1, bits):
+        io_level(level)
+    io_start(0)
+    io_core(c, mine).start()
+    start_chan(1)
+    for n in (4, 5, 6, 7):
+        shelve(n)
+    pieces_start()
     mix_prepare()
-
-    for tick in range(bits + 2):
+    taps_own.wait()
+    for off in range(1, chans):
+        taps_copy(off, True).wait_recv()
+    copy = pltpu.make_async_copy(taps_all, taps_v, taps_sem)
+    copy.start()
+    copy.wait()
+    mix_some(0)
+
+    settled = 2 * (chans - 1)
+    for tick in range(settled):
         start_chan(tick + 2)
         first_level(tick)
         for level in range(1, bits - 1):
@@ -951,12 +1061,17 @@
             arrived(tick - bits)
         if tick == 1:
             pieces_lift()
-    taps_own.wait()
-    for off in range(1, chans):
-        taps_copy(off, True).wait_recv()
-    mix()
-
-    @pl.loop(bits + 2, last + bits + 2)
+        if tick % 2 == 0:
+            io_arrive(tick // 2)
+        else:
+            mix_some(tick // 2 + 1)
+    mix_finish()
+
+    def done_by(tick):
+        some = jnp.minimum(2 * (tick - settled + 1), tick - bits + 1)
+        return jnp.minimum(jnp.maximum(some, 0), TILES)
+
+    @pl.loop(settled, TILES + bits)
     def _(tick):
         @pl.when(tick + 2 <= last)
         def _():
@@ -976,15 +1091,17 @@
         def _():
             to_core(tick - bits + 1)
 
-        @pl.when(tick - bits <= last)
-        def _():
-            arrived(tick - bits)
-            for copy in loads(tick - bits - 2):
+        arrived(tick - bits)
+        first = done_by(tick - 1)
+
+        @pl.when((tick == settled) | (first >= tick - bits))
+        def _():
+            for copy in loads(first):
                 copy.start()
 
-        @pl.when(tick - bits - 3 >= 0)
-        def _():
-            feed_forward(tick - bits - 3)
+        @pl.loop(first, done_by(tick))
+        def _(t):
+            feed_forward(t, tick - bits)
 
     for s in range(held):
         here = pl.ds(s * (size + HEAD) + HEAD, size)
@@ -995,10 +1112,9 @@
     pieces_finish()
     for off in range(1, chans):
         taps_copy(off, False).wait_send()
-    sent(0)
-    sent(1)
-
-    @pl.loop(2, last + 1)
+    io_sent()
+
+    @pl.loop(0, last + 1)
     def _(k):
         sent(k)
 
@@ -1011,8 +1127,7 @@
     tail = (PIECE, block)
     shape = jax.ShapeDtypeStruct
     outs = [
-        shape((chans, seqs, block, 3 * part), BF16),
-        shape((chans, seqs, block, part), BF16),
+        shape((chans, seqs // 2, 2, block, 4 * part), BF16),
         shape((TILES, chans, seqs, 3, block, LANES), BF16),
         shape((chans, 8, part), F32),
         shape((PIECES // seqs, seqs) + tail, BF16),
@@ -1022,21 +1137,27 @@
     outs.append(shape((3, PIECES, TILES, UNIT, width), BF16))
     outs += [shape((rows, width), F32)] * 4 + [shape((own_count, width), BF16)]
     dma = pltpu.SemaphoreType.DMA
-    count = TILES + 2
+    count = TILES
     vmem = pltpu.VMEM
     found = call(
         functools.partial(forward_kernel, seqs, chans, held),
         outs,
         [pl.ANY] * 10 + [vmem] + [pl.ANY] * 2 + [vmem] * 2,
-        [pl.ANY] * 8 + [vmem] * 5,
+        [pl.ANY] * 7 + [vmem] * 5,
         [
-            vmem((block, 3 * part), BF16),
-            vmem((block, part), BF16),
+            vmem((block, 4 * part), BF16),
             vmem((TILES, 3, block, LANES), BF16),
             vmem((8, part), F32),
             vmem((chans, PER_CHAN) + tail, BF16),
             vmem((2, block, TILES * LANES), F32),
             dma((2, 4)),
+            dma(()),
+            dma((2, seqs // 2 - 1)),
+            dma((2, seqs // 2 - 1)),
+            dma((chans,)),
+            dma((chans,)),
+            dma((2, chans - 1)),
+            dma((2, chans - 1)),
             vmem((rows, width), BF16),
             vmem((own_count, width), BF16),
             vmem((3, held, HEAD, width), F32),
@@ -1053,8 +1174,7 @@
             vmem((own_count, hidden), BF16),
             vmem((own_count, hidden), BF16),
             vmem((own_count, hidden), BF16),
-            vmem((2, seqs, block, 3 * part), BF16),
-            vmem((2, seqs, block, part), BF16),
+            vmem((seqs // 2, 2, block, 4 * part), BF16),
             vmem((chans, 8, part), F32),
             vmem((2, 3, seqs, block, hidden), BF16),
             vmem((2, 3, PIECES, UNIT, width), BF16),
@@ -1073,7 +1193,7 @@
             dma((seqs,)),
             dma((chans,)),
             dma((PIECES // seqs,)),
-            dma((2, 2)),
+            dma(()),
             dma(()),
             dma(()),
             dma((2, 3, chans)),
@@ -1095,9 +1215,9 @@
 
 def backward_kernel(
     seqs, chans, held,
-    ffn_g, in_full, out_full, streams, block_own,
+    ffn_g, io_full, streams, block_own,
     tokens, residual, second_grad, cotangent, keeps, gains, taps,
-    result, total, input_grad, io_g, blocks, *refs
+    result, total, input_grad, io_g, blocks, input_blocks, *refs
 ):
     bits = seqs.bit_length() - 1
     levels = bits - 1
@@ -1307,8 +1427,12 @@
 
     def mix_loads(j):
         return [
-            pltpu.make_async_copy(in_full.at[j], in_v, mix_sem.at[0]),
-            pltpu.make_async_copy(out_full.at[j], out_v, mix_sem.at[1]),
+            pltpu.make_async_copy(
+                io_full.at[j, :, :, :, pl.ds(0, 3 * width)], in_v, mix_sem.at[0]
+            ),
+            pltpu.make_async_copy(
+                io_full.at[j, :, :, :, pl.ds(3 * width, width)], out_v, mix_sem.at[1]
+            ),
             pltpu.make_async_copy(streams.at[j], stream, mix_sem.at[2]),
         ]
 
@@ -1422,7 +1546,8 @@
 
     spread_out = parts == 4
     mix_first, mix_last = (1, 3 * parts - 2) if spread_out else (-1, -1)
-    relay = Relay(chans, block_own, blocks, relay_sems)
+    relay = Relay(chans, block_own, blocks, relay_sems[:3])
+    input_relay = Relay(chans, input_grad, input_blocks, relay_sems[3:])
     for copy in mix_loads(0):
         copy.start()
     begin(0)
@@ -1483,11 +1608,16 @@
             def _():
                 relay.step(step)
 
-    relay.finish()
+        @pl.when(tick == mix_last + 6)
+        def _():
+            input_relay.step(0)
+
+    relay.finish(range(chans - 1))
+    input_relay.finish([0])
 
 
 def backward_pass(
-    seqs, chans, held, ffn_g, in_full, out_full, streams, block_own, tokens, residual, second_grad,
+    seqs, chans, held, ffn_g, io_full, streams, block_own, tokens, residual, second_grad,
     cotangent, keeps, gains, taps,
 ):
     dma, vmem, shape = pltpu.SemaphoreType.DMA, pltpu.VMEM, jax.ShapeDtypeStruct
@@ -1500,12 +1630,13 @@
     partners = (seqs * chans).bit_length() - 1
     rows, width = tokens.shape
     own_count = rows - held * HEAD
-    part = out_full.shape[-1]
+    part = io_full.shape[-1] // 4
     outs = [
         shape((parts, PIECE, D), BF16),
         shape((8, width), F32),
         shape((own_count, width), BF16),
         shape((parts, half_seqs, 2, PIECE, D), BF16),
+        shape((chans,) + block_own.shape, BF16),
         shape((chans,) + block_own.shape, BF16),
         shape((chunks, half_seqs, PIECE, D), BF16),
     ]
@@ -1516,7 +1647,7 @@
     return call(
         functools.partial(backward_kernel, seqs, chans, held),
         outs,
-        [pl.ANY] * 5 + [vmem] * 7,
+        [pl.ANY] * 4 + [vmem] * 7,
         [vmem] * 3 + [pl.ANY] * (len(outs) - 3),
         [
             *[vmem((size, PIECE, D), BF16) for size in sizes],
@@ -1534,8 +1665,8 @@
             vmem((rows, part), F32),
             vmem((own_count, width), F32),
             vmem((rows, 3 * part), F32),
-            vmem(in_full.shape[1:], BF16),
-            vmem(out_full.shape[1:], BF16),
+            vmem(io_full.shape[1:4] + (3 * part,), BF16),
+            vmem(io_full.shape[1:4] + (part,), BF16),
             vmem((4, 2, PIECE, D), BF16),
             dma((chunks,)),
             dma(()),
@@ -1551,13 +1682,14 @@
             dma((3,)),
             dma(()),
             *Relay.semaphores(chans),
+            *Relay.semaphores(chans),
         ],
         1,
         ffn_g.reshape(3, parts, half_seqs, 2, PIECE, D),
-        in_full, out_full, streams, block_own, tokens, residual, second_grad, cotangent, keeps, gains,
+        io_full, streams, block_own, tokens, residual, second_grad, cotangent, keeps, gains,
         taps,
         vmem=62,
-    )[:5]
+    )[:6]
 
 
 def shifted(value, axes, by):
@@ -1691,14 +1823,14 @@
     keeps = jnp.concatenate([following, gap, share(local_keeps, c * sub, sub)], axis=1).reshape(-1, 2)
 
     (
-        in_full, out_full, _, taps, moments_held, _, streams, ffn_grads,
+        io_full, _, taps, moments_held, _, streams, ffn_grads,
         token_rows, upstream_rows, residual, second_grad, block_out,
     ) = forward_pass(
         seqs, chans, weights, moments, filter_weight, tokens, cotangent, keeps, norm_gains
     )
     moments_held = moments_held.transpose(0, 2, 1, 3).reshape(-1, D)
-    grads_held, small, input_grad, _, block_out = backward_pass(
-        seqs, chans, seq_total, ffn_grads, in_full, out_full, streams, block_out, token_rows, residual,
+    grads_held, small, _, _, block_out, input_grad = backward_pass(
+        seqs, chans, seq_total, ffn_grads, io_full, streams, block_out, token_rows, residual,
         second_grad, upstream_rows, keeps, norm_gains, taps,
     )
 

time: 674 us -> 695 us (1.031)
  the two profiles are of different devices: /device:TPU:0 before, /device:TPU:9 now
where the time goes in v2:
time: 695 us; the launch traced here: 686 us
  Pallas kernels  670 us (96%)
  local copies, waits for them, and re-layouts  7.1 us (1%)
    pallas_call x3, Pallas kernels, call(): pl.pallas_call(kernel, out_shape=outs, in_specs=[pl.BlockSpec(memory_spac...  652 us
    pallas_call x1, Pallas kernels, last_pass(): pl.pallas_call(last_kernel, grid=(held,), out_shape=outs, in_specs=[low]...  17.6 us
  transfers between devices with their start and end apart: 1, of which 1 were waited for; matrix products, arithmetic and copies ran while one was open for 0% of the time, Pallas kernels for 0%

profile of v2, /device:TPU:9, one launch (start us, length us, event | category | flops | bytes accessed | tf_op | source)
XLA Modules:
  0.0 686.1 jit_solution(13579922763212354229)
XLA Ops:
  0.7 0.7 compare_bitcast_fusion.1
  1.4 2.6 collective-permute-start
  4.1 0.1 pad.2.clone
  4.1 2.3 collective-permute-done
  6.4 0.1 dynamic-slice_select_fusion
  6.5 0.1 pad_maximum_fusion
  6.6 1.0 copy.49
  7.6 252.6 %shard_map.322 = (bf16[4,4,2,128,1024]{4,3,2,1,0:T(8,128)(2,1)}, bf16[9,4,8,3,128,128]{5,4,3,2,1,0:T(8,128)(2,1)}, f32[4,8,256]{2,1,0:T(8,128)}, bf16[4,8,144,12...) custom-call(f32[3,128,256]{2,1,0:T(8,128)} %bitcast.28, ...), custom_call_target="tpu_custom_call" | custom-call | tf_op jit(solution)/shard_map/pallas_call | solution.py:74
  260.2 1.6 copy.50
  261.7 0.3 copy.53
  262.1 0.0 copy-start.3
  262.1 0.0 copy-start.5
  262.1 0.0 copy-start.6
  262.1 211.2 %shard_map.323 = (bf16[4,144,1024]{2,1,0:T(8,128)(2,1)}, f32[8,1024]{1,0:T(8,128)}, bf16[768,1024]{1,0:T(8,128)(2,1)}, bf16[4,4,2,144,1024]{4,3,2,1,0:T(8,128)(2...) custom-call(bf16[3,4,4,2,144,1024]{5,4,3,2,1,0:T(8,128)(2,1)} %bitca, ...), custom_call_target="tpu_custom_call" | custom-call | tf_op jit(solution)/shard_map/pallas_call | solution.py:74
  473.3 0.0 copy-start.4
  473.3 0.0 copy-start.7
  473.3 0.0 copy-start.8
  473.4 0.8 slice.19
  474.1 0.0 copy-done.3
  474.1 0.0 copy-done.5
  474.1 0.0 copy-done.6
  474.1 1.4 divide_subtract_fusion
  475.5 0.0 copy-start.2
  475.5 1.3 copy-done.2
  476.8 188.5 %shard_map.324 = (bf16[4,8,144,128]{3,2,1,0:T(8,128)(2,1)S(1)}, bf16[4,8,144,128]{3,2,1,0:T(8,128)(2,1)S(1)}, bf16[4,768,1024]{2,1,0:T(8,128)(2,1)}) custom-call(bf16[576,1024]{1,0:T(8,128)(2,1)S(1)} %bitcast.21, bf16[576,1024]{1,0:T(8,128)(2,1)S(1)} %bitcast.20, bf16[4,768,1024]{2,1,0:T(8,128)(2,1)} %get-tuple-element.59._), custom_call_target="tpu_custom_call", output_to_operand_aliasing={{2}: (2, {})} | custom-call | tf_op jit(solution)/shard_map/pallas_call | solution.py:74
  665.3 0.0 copy-start
  665.3 1.0 copy-done
  666.3 0.0 copy-start.1
  666.3 1.0 copy-done.1
  667.4 0.0 copy-done.4
  667.4 0.0 copy-done.7
  667.4 0.0 copy-done.8
  667.4 0.6 divide_subtract_fusion.1
  668.0 17.6 %shard_map.325 = (f32[6,512,1024]{2,1,0:T(8,128)}, f32[6,512,1024]{2,1,0:T(8,128)}, f32[3,128,256]{2,1,0:T(8,128)}, f32[3,128,256]{2,1,0:T(8,128)}, f32[128,256]...) custom-call(bf16[4,6,128,1024]{3,2,1,0:T(8,128)(2,1)} %bitcast.24, ...), custom_call_target="tpu_custom_call" | custom-call | tf_op jit(solution)/shard_map/pallas_call | solution.py:1767
  (6 shorter events, 0.0 us)
Async XLA Ops:
  1.4 5.0 collective-permute-start
  262.1 212.1 %copy-start.3 = (f32[2,1024]{1,0:T(2,128)S(1)}, f32[2,1024]{1,0:T(2,128)}, u32[]{:S(2)}) copy-start(f32[2,1024]{1,0:T(2,128)} %gains.1) | copy-start | bytes 24580
  262.1 212.1 %copy-start.5 = (f32[2,1024]{1,0:T(2,128)S(1)}, f32[2,1024]{1,0:T(2,128)}, u32[]{:S(2)}) copy-start(f32[2,1024]{1,0:T(2,128)} %param.29) | copy-start | bytes 24580
  262.1 212.0 %copy-start.6 = (f32[2,1024]{1,0:T(2,128)S(1)}, f32[2,1024]{1,0:T(2,128)}, u32[]{:S(2)}) copy-start(f32[2,1024]{1,0:T(2,128)} %param.30) | copy-start | bytes 24580
  473.3 194.1 %copy-start.4 = (f32[3,256]{1,0:T(4,128)S(1)}, f32[3,256]{1,0:T(4,128)}, u32[]{:S(2)}) copy-start(f32[3,256]{1,0:T(4,128)} %refs_10_.1) | copy-start | bytes 9220
  473.3 194.0 %copy-start.7 = (f32[3,256]{1,0:T(4,128)S(1)}, f32[3,256]{1,0:T(4,128)}, u32[]{:S(2)}) copy-start(f32[3,256]{1,0:T(4,128)} %param.31) | copy-start | bytes 9220
  473.3 194.0 %copy-start.8 = (f32[3,256]{1,0:T(4,128)S(1)}, f32[3,256]{1,0:T(4,128)}, u32[]{:S(2)}) copy-start(f32[3,256]{1,0:T(4,128)} %param.32) | copy-start | bytes 9220
  475.5 1.3 copy-start.2
  665.3 1.0 copy-start
  666.3 1.0 copy-start.1

commit v3 on v1

--- a/solution.py
+++ b/solution.py
@@ -70,13 +70,14 @@
     return order if half == 0 else order[::-1]
 
 
-def call(kernel, outs, in_spaces, out_spaces, scratch, ident, *args, vmem=48):
+def call(kernel, outs, in_spaces, out_spaces, scratch, ident, *args, vmem=48, aliases=None):
     return pl.pallas_call(
         kernel,
         out_shape=outs,
         in_specs=[pl.BlockSpec(memory_space=space) for space in in_spaces],
         out_specs=jax.tree.map(lambda space: pl.BlockSpec(memory_space=space), out_spaces),
         scratch_shapes=scratch,
+        input_output_aliases=aliases or {},
         compiler_params=pltpu.CompilerParams(
             collective_id=ident, has_side_effects=True, vmem_limit_bytes=vmem * 1024 * 1024
         ),
@@ -208,14 +209,14 @@
             @pl.when(comes)
             def _():
                 remote(
-                    self.own, self.blocks.at[block], self.send.at[side, hop], self.recv.at[side, hop],
-                    chan=c - 1 + 2 * side,
+                    self.blocks.at[block], self.blocks.at[block],
+                    self.send.at[side, hop], self.recv.at[side, hop], chan=c - 1 + 2 * side,
                 ).wait_recv()
 
-    def step(self, hop):
+    def step(self, hop, first=False):
         if hop == 0:
             self.keeping().start()
-        else:
+        elif not first:
             self.await_hop(hop - 1)
         for sends, copy in self.copies(hop):
 
@@ -223,10 +224,11 @@
             def _():
                 copy.start()
 
-    def finish(self):
-        self.await_hop(self.chans - 2)
-        self.keeping().wait()
-        for hop in range(self.chans - 1):
+    def finish(self, hops):
+        self.await_hop(hops[-1])
+        if 0 in hops:
+            self.keeping().wait()
+        for hop in hops:
             for sends, copy in self.copies(hop):
 
                 @pl.when(sends)
@@ -252,7 +254,7 @@
 
 
 def ortho_kernel(
-    seqs, chans, grad, moment, input_grad, grad_home, ortho_home, input_blocks,
+    seqs, chans, grad, moment, _, grad_home, ortho_home, input_blocks,
     out, cut_grad, cut_ortho, between_grad, between_ortho,
     part, own, swapped, paired, parts, sums, gram, poly, half_way,
     x_send, x_recv, s_send, s_recv, g_send, g_recv, f_send, f_recv, *home_sems
@@ -269,7 +271,7 @@
     )
     home_grad = Homeward(seqs, chans, cut_grad, grad_home, between_grad, home_sems[:6])
     home_ortho = Homeward(seqs, chans, cut_ortho, ortho_home, between_ortho, home_sems[6:12])
-    relay = Relay(chans, input_grad, input_blocks, home_sems[12:])
+    relay = Relay(chans, None, input_blocks, home_sems[12:])
     columns = out.shape[0]
     slab = PIECE
 
@@ -282,7 +284,7 @@
 
     for at in range(columns // slab):
         home_grad.drop(at)
-    relay.step(0)
+    relay.step(1, first=True)
 
     apart = c == chans - 1
 
@@ -381,8 +383,6 @@
             share(peer).wait_send()
         for pair in [h] + peers:
             forward(pair).wait_send()
-        if turn == 1:
-            relay.step(2)
 
         scale = jnp.ones((1, 1), F32)
         if turn == 0:
@@ -444,21 +444,21 @@
 
         if turn == 0:
             home_grad.spread()
-            relay.step(1)
+            relay.step(2)
 
     home_ortho.spread()
     home_grad.finish()
-    relay.finish()
+    relay.finish(range(1, chans - 1))
     home_ortho.finish()
 
 
-def orthogonalize(seqs, chans, grad, moment, input_grad):
+def orthogonalize(seqs, chans, grad, moment, input_blocks):
     dma = pltpu.SemaphoreType.DMA
     count, block, held = seqs // 2, D // seqs, PIECES // seqs
     return call(
         functools.partial(ortho_kernel, seqs, chans),
         [jax.ShapeDtypeStruct((chans, PER_CHAN, PIECE, block), BF16)] * 2
-        + [jax.ShapeDtypeStruct((chans,) + input_grad.shape, BF16)],
+        + [jax.ShapeDtypeStruct(input_blocks.shape, BF16)],
         [pltpu.VMEM] * 2 + [pl.ANY],
         [pl.ANY] * 3,
         [
@@ -485,7 +485,8 @@
         2,
         grad,
         moment,
-        input_grad,
+        input_blocks,
+        aliases={2: 2},
     )
 
 
@@ -791,6 +792,31 @@
             normed[here] = (values * row_scale(values) * gains[0:1]).astype(BF16)
             residual[here] = values
 
+    def transfers(tick):
+        @pl.when(tick + 2 <= last)
+        def _():
+            start_chan(tick + 2)
+
+        @pl.when(tick <= last)
+        def _():
+            first_level(tick)
+
+        for level in range(1, bits - 1):
+
+            @pl.when(tick - level <= last)
+            def _():
+                next_level(tick - level, level)
+
+        @pl.when(tick - bits + 1 <= last)
+        def _():
+            to_core(tick - bits + 1)
+
+        @pl.when(tick - bits <= last)
+        def _():
+            arrived(tick - bits)
+            for copy in loads(tick - bits - 2):
+                copy.start()
+
     def mix():
         for copy in mix_loads(0):
             copy.start()
@@ -824,6 +850,10 @@
             stream_out(j).start()
             for here in tiles:
                 residual[here] += contract_last(mixed[here], out_w)
+
+            @pl.when(j == 1)
+            def _():
+                transfers(bits + 2)
 
         for at, here in enumerate(tiles):
             values = residual[here]
@@ -932,7 +962,6 @@
             for t in range(TILES):
                 block = shelf[slot, :, t * LANES : (t + 1) * LANES].T.astype(BF16)
                 packed[m, :, t * UNIT : (t + 1) * UNIT] = block.reshape(PER_CHAN, UNIT, -1)
-    pieces_start()
     taps_own = pltpu.make_async_copy(taps, taps_all.at[c], t_own)
     taps_own.start()
     for off in range(1, chans):
@@ -949,42 +978,24 @@
             to_core(tick - bits + 1)
         if tick >= bits:
             arrived(tick - bits)
-        if tick == 1:
-            pieces_lift()
     taps_own.wait()
     for off in range(1, chans):
         taps_copy(off, True).wait_recv()
     mix()
 
-    @pl.loop(bits + 2, last + bits + 2)
+    @pl.loop(bits + 3, last + bits + 2)
     def _(tick):
-        @pl.when(tick + 2 <= last)
-        def _():
-            start_chan(tick + 2)
-
-        @pl.when(tick <= last)
-        def _():
-            first_level(tick)
-
-        for level in range(1, bits - 1):
-
-            @pl.when(tick - level <= last)
-            def _():
-                next_level(tick - level, level)
-
-        @pl.when(tick - bits + 1 <= last)
-        def _():
-            to_core(tick - bits + 1)
-
-        @pl.when(tick - bits <= last)
-        def _():
-            arrived(tick - bits)
-            for copy in loads(tick - bits - 2):
-                copy.start()
-
-        @pl.when(tick - bits - 3 >= 0)
-        def _():
-            feed_forward(tick - bits - 3)
+        transfers(tick)
+
+        @pl.when(tick == last)
+        def _():
+            pieces_start()
+
+        @pl.when(tick == last + 2)
+        def _():
+            pieces_lift()
+
+        feed_forward(tick - bits - 3)
 
     for s in range(held):
         here = pl.ds(s * (size + HEAD) + HEAD, size)
@@ -1097,7 +1108,7 @@
     seqs, chans, held,
     ffn_g, in_full, out_full, streams, block_own,
     tokens, residual, second_grad, cotangent, keeps, gains, taps,
-    result, total, input_grad, io_g, blocks, *refs
+    result, total, input_grad, io_g, blocks, input_blocks, *refs
 ):
     bits = seqs.bit_length() - 1
     levels = bits - 1
@@ -1422,7 +1433,8 @@
 
     spread_out = parts == 4
     mix_first, mix_last = (1, 3 * parts - 2) if spread_out else (-1, -1)
-    relay = Relay(chans, block_own, blocks, relay_sems)
+    relay = Relay(chans, block_own, blocks, relay_sems[:3])
+    input_relay = Relay(chans, input_grad, input_blocks, relay_sems[3:])
     for copy in mix_loads(0):
         copy.start()
     begin(0)
@@ -1483,7 +1495,12 @@
             def _():
                 relay.step(step)
 
-    relay.finish()
+        @pl.when(tick == mix_last + 6)
+        def _():
+            input_relay.step(0)
+
+    relay.finish(range(chans - 1))
+    input_relay.finish([0])
 
 
 def backward_pass(
@@ -1506,6 +1523,7 @@
         shape((8, width), F32),
         shape((own_count, width), BF16),
         shape((parts, half_seqs, 2, PIECE, D), BF16),
+        shape((chans,) + block_own.shape, BF16),
         shape((chans,) + block_own.shape, BF16),
         shape((chunks, half_seqs, PIECE, D), BF16),
     ]
@@ -1551,13 +1569,14 @@
             dma((3,)),
             dma(()),
             *Relay.semaphores(chans),
+            *Relay.semaphores(chans),
         ],
         1,
         ffn_g.reshape(3, parts, half_seqs, 2, PIECE, D),
         in_full, out_full, streams, block_own, tokens, residual, second_grad, cotangent, keeps, gains,
         taps,
         vmem=62,
-    )[:5]
+    )[:6]
 
 
 def shifted(value, axes, by):
@@ -1697,7 +1716,7 @@
         seqs, chans, weights, moments, filter_weight, tokens, cotangent, keeps, norm_gains
     )
     moments_held = moments_held.transpose(0, 2, 1, 3).reshape(-1, D)
-    grads_held, small, input_grad, _, block_out = backward_pass(
+    grads_held, small, _, _, block_out, input_grad = backward_pass(
         seqs, chans, seq_total, ffn_grads, in_full, out_full, streams, block_out, token_rows, residual,
         second_grad, upstream_rows, keeps, norm_gains, taps,
     )

time: 674 us -> 680 us (level); the launches traced: 670 us -> 669 us
  no operation moved by 1% of the time
where the time goes in v3:
time: 680 us; the launch traced here: 669 us
  Pallas kernels  655 us (96%)
  local copies, waits for them, and re-layouts  7.1 us (1%)
    pallas_call x3, Pallas kernels, call(): pl.pallas_call(kernel, out_shape=outs, in_specs=[pl.BlockSpec(memory_spac...  637 us
    pallas_call x1, Pallas kernels, last_pass(): pl.pallas_call(last_kernel, grid=(held,), out_shape=outs, in_specs=[low]...  17.6 us
  transfers between devices with their start and end apart: 1, of which 1 were waited for; matrix products, arithmetic and copies ran while one was open for 0% of the time, Pallas kernels for 0%

profile of v3, /device:TPU:0, one launch (start us, length us, event | category | flops | bytes accessed | tf_op | source)
XLA Modules:
  0.0 669.1 jit_solution(4372639163103280818)
XLA Ops:
  0.7 0.7 compare_bitcast_fusion.1
  1.4 1.3 collective-permute-start
  2.8 0.1 pad.2.clone
  2.8 1.6 collective-permute-done
  4.5 0.1 dynamic-slice_select_fusion
  4.6 0.1 pad_maximum_fusion
  4.6 1.0 copy.49
  5.6 243.0 %shard_map.322 = (bf16[4,8,128,768]{3,2,1,0:T(8,128)(2,1)}, bf16[4,8,128,256]{3,2,1,0:T(8,128)(2,1)}, bf16[9,4,8,3,128,128]{5,4,3,2,1,0:T(8,128)(2,1)}, f32[4,8,...) custom-call(f32[3,128,256]{2,1,0:T(8,128)} %bitcast.28, ...), custom_call_target="tpu_custom_call" | custom-call | tf_op jit(solution)/shard_map/pallas_call | solution.py:74
  248.7 1.6 copy.50
  250.2 0.3 copy.53
  250.6 0.0 copy-start.3
  250.6 0.0 copy-start.5
  250.6 0.0 copy-start.6
  250.6 232.7 %shard_map.323 = (bf16[4,144,1024]{2,1,0:T(8,128)(2,1)}, f32[8,1024]{1,0:T(8,128)}, bf16[768,1024]{1,0:T(8,128)(2,1)}, bf16[4,4,2,144,1024]{4,3,2,1,0:T(8,128)(2...) custom-call(bf16[3,4,4,2,144,1024]{5,4,3,2,1,0:T(8,128)(2,1)} %bitca, ...), custom_call_target="tpu_custom_call" | custom-call | tf_op jit(solution)/shard_map/pallas_call | solution.py:74
  483.4 0.0 copy-start.4
  483.4 0.0 copy-start.7
  483.4 0.0 copy-start.8
  483.4 0.8 slice.19
  484.2 0.0 copy-done.3
  484.2 0.0 copy-done.5
  484.2 0.0 copy-done.6
  484.2 1.4 divide_subtract_fusion
  485.6 0.0 copy-start.2
  485.6 1.3 copy-done.2
  486.8 161.5 %shard_map.324 = (bf16[4,8,144,128]{3,2,1,0:T(8,128)(2,1)S(1)}, bf16[4,8,144,128]{3,2,1,0:T(8,128)(2,1)S(1)}, bf16[4,768,1024]{2,1,0:T(8,128)(2,1)}) custom-call(bf16[576,1024]{1,0:T(8,128)(2,1)S(1)} %bitcast.21, bf16[576,1024]{1,0:T(8,128)(2,1)S(1)} %bitcast.20, bf16[4,768,1024]{2,1,0:T(8,128)(2,1)} %get-tuple-element.61._), custom_call_target="tpu_custom_call", output_to_operand_aliasing={{2}: (2, {})} | custom-call | tf_op jit(solution)/shard_map/pallas_call | solution.py:74
  648.3 0.0 copy-start
  648.3 1.0 copy-done
  649.4 0.0 copy-start.1
  649.4 1.0 copy-done.1
  650.4 0.0 copy-done.4
  650.4 0.0 copy-done.7
  650.4 0.0 copy-done.8
  650.4 0.6 divide_subtract_fusion.1
  651.0 17.6 %shard_map.325 = (f32[6,512,1024]{2,1,0:T(8,128)}, f32[6,512,1024]{2,1,0:T(8,128)}, f32[3,128,256]{2,1,0:T(8,128)}, f32[3,128,256]{2,1,0:T(8,128)}, f32[128,256]...) custom-call(bf16[4,6,128,1024]{3,2,1,0:T(8,128)(2,1)} %bitcast.24, ...), custom_call_target="tpu_custom_call" | custom-call | tf_op jit(solution)/shard_map/pallas_call | solution.py:1654
  (6 shorter events, 0.0 us)
Async XLA Ops:
  1.4 3.1 collective-permute-start
  250.6 233.6 %copy-start.3 = (f32[2,1024]{1,0:T(2,128)S(1)}, f32[2,1024]{1,0:T(2,128)}, u32[]{:S(2)}) copy-start(f32[2,1024]{1,0:T(2,128)} %gains.1) | copy-start | bytes 24580
  250.6 233.6 %copy-start.5 = (f32[2,1024]{1,0:T(2,128)S(1)}, f32[2,1024]{1,0:T(2,128)}, u32[]{:S(2)}) copy-start(f32[2,1024]{1,0:T(2,128)} %param.29) | copy-start | bytes 24580
  250.6 233.6 %copy-start.6 = (f32[2,1024]{1,0:T(2,128)S(1)}, f32[2,1024]{1,0:T(2,128)}, u32[]{:S(2)}) copy-start(f32[2,1024]{1,0:T(2,128)} %param.30) | copy-start | bytes 24580
  483.4 167.0 %copy-start.4 = (f32[3,256]{1,0:T(4,128)S(1)}, f32[3,256]{1,0:T(4,128)}, u32[]{:S(2)}) copy-start(f32[3,256]{1,0:T(4,128)} %refs_10_.1) | copy-start | bytes 9220
  483.4 167.0 %copy-start.7 = (f32[3,256]{1,0:T(4,128)S(1)}, f32[3,256]{1,0:T(4,128)}, u32[]{:S(2)}) copy-start(f32[3,256]{1,0:T(4,128)} %param.31) | copy-start | bytes 9220
  483.4 167.0 %copy-start.8 = (f32[3,256]{1,0:T(4,128)S(1)}, f32[3,256]{1,0:T(4,128)}, u32[]{:S(2)}) copy-start(f32[3,256]{1,0:T(4,128)} %param.32) | copy-start | bytes 9220
  485.6 1.3 copy-start.2
  648.3 1.0 copy-start
  649.4 1.0 copy-start.1

commit v4 on v1

--- a/solution.py
+++ b/solution.py
@@ -369,6 +369,8 @@
         sums[1] = jnp.where(apart, groups[1], both).astype(BF16)
         for peer in peers:
             share(peer).start()
+        if turn == 1:
+            relay.step(2)
         gram[block_at(h, core)] = sums[mine]
         forward(h).start()
         for peer in peers:
@@ -381,8 +383,8 @@
             share(peer).wait_send()
         for pair in [h] + peers:
             forward(pair).wait_send()
-        if turn == 1:
-            relay.step(2)
+        if turn == 0:
+            relay.step(1)
 
         scale = jnp.ones((1, 1), F32)
         if turn == 0:
@@ -444,7 +446,6 @@
 
         if turn == 0:
             home_grad.spread()
-            relay.step(1)
 
     home_ortho.spread()
     home_grad.finish()
@@ -791,6 +792,31 @@
             normed[here] = (values * row_scale(values) * gains[0:1]).astype(BF16)
             residual[here] = values
 
+    def transfers(tick):
+        @pl.when(tick + 2 <= last)
+        def _():
+            start_chan(tick + 2)
+
+        @pl.when(tick <= last)
+        def _():
+            first_level(tick)
+
+        for level in range(1, bits - 1):
+
+            @pl.when(tick - level <= last)
+            def _():
+                next_level(tick - level, level)
+
+        @pl.when(tick - bits + 1 <= last)
+        def _():
+            to_core(tick - bits + 1)
+
+        @pl.when(tick - bits <= last)
+        def _():
+            arrived(tick - bits)
+            for copy in loads(tick - bits - 2):
+                copy.start()
+
     def mix():
         for copy in mix_loads(0):
             copy.start()
@@ -824,6 +850,10 @@
             stream_out(j).start()
             for here in tiles:
                 residual[here] += contract_last(mixed[here], out_w)
+
+            @pl.when(j == 1)
+            def _():
+                transfers(bits + 2)
 
         for at, here in enumerate(tiles):
             values = residual[here]
@@ -956,35 +986,10 @@
         taps_copy(off, True).wait_recv()
     mix()
 
-    @pl.loop(bits + 2, last + bits + 2)
+    @pl.loop(bits + 3, last + bits + 2)
     def _(tick):
-        @pl.when(tick + 2 <= last)
-        def _():
-            start_chan(tick + 2)
-
-        @pl.when(tick <= last)
-        def _():
-            first_level(tick)
-
-        for level in range(1, bits - 1):
-
-            @pl.when(tick - level <= last)
-            def _():
-                next_level(tick - level, level)
-
-        @pl.when(tick - bits + 1 <= last)
-        def _():
-            to_core(tick - bits + 1)
-
-        @pl.when(tick - bits <= last)
-        def _():
-            arrived(tick - bits)
-            for copy in loads(tick - bits - 2):
-                copy.start()
-
-        @pl.when(tick - bits - 3 >= 0)
-        def _():
-            feed_forward(tick - bits - 3)
+        transfers(tick)
+        feed_forward(tick - bits - 3)
 
     for s in range(held):
         here = pl.ds(s * (size + HEAD) + HEAD, size)

time: 674 us -> 672 us (level)
  no operation moved by 1% of the time
where the time goes in v4:
time: 672 us; the launch traced here: 666 us
  Pallas kernels  654 us (97%)
    pallas_call x3, Pallas kernels, call(): pl.pallas_call(kernel, out_shape=outs, in_specs=[pl.BlockSpec(memory_spac...  636 us
    pallas_call x1, Pallas kernels, last_pass(): pl.pallas_call(last_kernel, grid=(held,), out_shape=outs, in_specs=[low]...  17.6 us
  transfers between devices with their start and end apart: 1, of which 1 were waited for; matrix products, arithmetic and copies ran while one was open for 0% of the time, Pallas kernels for 0%

profile of v4, /device:TPU:0, one launch (start us, length us, event | category | flops | bytes accessed | tf_op | source)
XLA Modules:
  0.0 665.5 jit_solution(7118729580438831476)
XLA Ops:
  0.7 0.7 compare_bitcast_fusion.1
  1.4 1.3 collective-permute-start
  2.8 0.1 pad.2.clone
  2.8 1.6 collective-permute-done
  4.5 0.1 dynamic-slice_select_fusion
  4.6 0.1 pad_maximum_fusion
  4.6 1.0 copy.48
  5.6 229.9 %shard_map.322 = (bf16[4,8,128,768]{3,2,1,0:T(8,128)(2,1)}, bf16[4,8,128,256]{3,2,1,0:T(8,128)(2,1)}, bf16[9,4,8,3,128,128]{5,4,3,2,1,0:T(8,128)(2,1)}, f32[4,8,...) custom-call(f32[3,128,256]{2,1,0:T(8,128)} %bitcast.28, ...), custom_call_target="tpu_custom_call" | custom-call | tf_op jit(solution)/shard_map/pallas_call | solution.py:74
  235.5 0.0 copy-start.3
  235.5 219.7 %shard_map.323 = (bf16[4,144,1024]{2,1,0:T(8,128)(2,1)}, f32[8,1024]{1,0:T(8,128)}, bf16[768,1024]{1,0:T(8,128)(2,1)}, bf16[4,4,2,144,1024]{4,3,2,1,0:T(8,128)(2...) custom-call(bf16[3,4,4,2,144,1024]{5,4,3,2,1,0:T(8,128)(2,1)} %bitca, ...), custom_call_target="tpu_custom_call" | custom-call | tf_op jit(solution)/shard_map/pallas_call | solution.py:74
  455.2 0.0 copy-start.4
  455.2 0.0 copy-start.6
  455.2 0.0 copy-start.7
  455.3 0.0 copy-start.2
  455.3 0.0 copy-start.5
  455.3 0.0 copy-start.8
  455.3 0.0 copy-start.9
  455.3 0.9 slice.19
  456.2 0.0 copy-done.3
  456.2 0.3 copy.49
  456.5 0.3 copy.52
  456.8 0.0 copy-done.4
  456.8 0.0 copy-done.6
  456.8 0.0 copy-done.7
  456.8 1.4 divide_subtract_fusion
  458.2 0.0 copy-done.2
  458.2 186.5 %shard_map.324 = (bf16[4,8,144,128]{3,2,1,0:T(8,128)(2,1)S(1)}, bf16[4,8,144,128]{3,2,1,0:T(8,128)(2,1)S(1)}, bf16[4,768,1024]{2,1,0:T(8,128)(2,1)}) custom-call(bf16[576,1024]{1,0:T(8,128)(2,1)S(1)} %bitcast.21, bf16[576,1024]{1,0:T(8,128)(2,1)S(1)} %bitcast.20, bf16[768,1024]{1,0:T(8,128)(2,1)} %get-tuple-element.61.input_grad), custom_call_target="tpu_custom_call" | custom-call | tf_op jit(solution)/shard_map/pallas_call | solution.py:74
  644.7 0.0 copy-start
  644.7 1.0 copy-done
  645.7 0.0 copy-start.1
  645.7 1.1 copy-done.1
  646.8 0.0 copy-done.5
  646.8 0.0 copy-done.8
  646.8 0.0 copy-done.9
  646.8 0.6 divide_subtract_fusion.1
  647.4 17.6 %shard_map.325 = (f32[6,512,1024]{2,1,0:T(8,128)}, f32[6,512,1024]{2,1,0:T(8,128)}, f32[3,128,256]{2,1,0:T(8,128)}, f32[3,128,256]{2,1,0:T(8,128)}, f32[128,256]...) custom-call(bf16[4,6,128,1024]{3,2,1,0:T(8,128)(2,1)} %bitcast.23, ...), custom_call_target="tpu_custom_call" | custom-call | tf_op jit(solution)/shard_map/pallas_call | solution.py:1640
  (6 shorter events, 0.0 us)
Async XLA Ops:
  1.4 3.1 collective-permute-start
  235.5 220.6 %copy-start.3 = (bf16[4,8,144,128]{3,2,1,0:T(8,128)(2,1)S(1)}, bf16[4,8,144,128]{3,2,1,0:T(8,128)(2,1)}, u32[]{:S(2)}) copy-start(bf16[4,8,144,128]{3,2,1,0:T(8,128)(2,1)} %get-tuple-element.60) | copy-start | bytes 3538948
  455.2 1.6 copy-start.4
  455.2 1.6 copy-start.6
  455.2 1.6 copy-start.7
  455.3 3.0 copy-start.2
  455.3 191.6 %copy-start.5 = (f32[3,256]{1,0:T(4,128)S(1)}, f32[3,256]{1,0:T(4,128)}, u32[]{:S(2)}) copy-start(f32[3,256]{1,0:T(4,128)} %refs_10_.1) | copy-start | bytes 9220
  455.3 191.6 %copy-start.8 = (f32[3,256]{1,0:T(4,128)S(1)}, f32[3,256]{1,0:T(4,128)}, u32[]{:S(2)}) copy-start(f32[3,256]{1,0:T(4,128)} %param.31) | copy-start | bytes 9220
  455.3 191.5 %copy-start.9 = (f32[3,256]{1,0:T(4,128)S(1)}, f32[3,256]{1,0:T(4,128)}, u32[]{:S(2)}) copy-start(f32[3,256]{1,0:T(4,128)} %param.32) | copy-start | bytes 9220
  644.7 1.0 copy-start
  645.7 1.1 copy-start.1
